TPU v7x, 32 devices: a whole 2x2x4 slice. The times are simulated.
32 devices in a mesh: seq: 32 (over z, y, x, core).
Axes of the slice: x: 2, y: 2, z: 4, core: 2. Of those that a mesh axis runs over, the one named last changes fastest.
Arguments:
- tokens: bfloat16 [1, 4096, 2048], P(None, 'seq'), may hold values from -6 to 6
- previous: float32 [1, 2, 2048], replicated, may hold values from -6 to 6
- initial_state: float32 [2048, 64], P('seq'), may hold values from -16 to 16
- mixing_weights: bfloat16 [2048, 10240], P('seq'), may hold values from -0.125 to 0.125
- lowrank_weights: bfloat16 [2048, 448], P('seq'), as said below
- vectors: float32 [2048, 16], P('seq'), as said below
- feedforward_weights: bfloat16 [2048, 16384], P('seq'), as said below
- cotangent: bfloat16 [1, 4096, 2048], P(None, 'seq'), may hold values from -6 to 6
Outputs:
- block_output: bfloat16 [1, 4096, 2048], P(None, 'seq')
- block_input_gradient: float32 [1, 4096, 2048], P(None, 'seq')
- initial_state_gradient: float32 [2048, 64], P('seq')
- mixing_gradient: float32 [2048, 10240], P('seq')
- lowrank_gradient: float32 [2048, 448], P('seq')
- vectors_gradient: float32 [2048, 16], P('seq')
- feedforward_gradient: float32 [2048, 16384], P('seq')
Inputs may be any that keep to these rules, and one draw needn't show every extreme that they name: `lowrank_weights`: column blocks drawn at their fan-in scale. `vectors`: gains positive, shift mixes between 0 and 1, decay base negative. `feedforward_weights`: column blocks drawn at their fan-in scale.
All inputs are finite; a program needn't handle non-finite values.
Results may differ from a plain program's by a relative error of at most 0.015.
Values may be sent and summed in bfloat16 or wider, within the bound.
No kernel may reach another device: no remote copies, remote signals or barrier semaphores. Data moves between devices by JAX's collectives and lax.ppermute only.
A program may use at most 512 MiB of HBM per device.

v0:
```python
import functools

import jax
import jax.numpy as jnp
from jax import lax
from jax.experimental import pallas as pl
from jax.experimental.pallas import tpu as pltpu
from jax.sharding import PartitionSpec as P

HEADS = 32
SPAN = 64
FF = 7168
RANK = 32
DRANK = 64
LN_EPS = 1e-05
GN_EPS = 0.00064

F32 = jnp.float32
BF16 = jnp.bfloat16
HI = lax.Precision.HIGHEST


def nn(a, b):
    return jnp.dot(a, b, preferred_element_type=F32)


def nt(a, b):
    return lax.dot_general(a, b, (((1,), (1,)), ((), ())), preferred_element_type=F32)


def tn(a, b):
    return lax.dot_general(a, b, (((0,), (0,)), ((), ())), preferred_element_type=F32)


def knn(a, b):
    return lax.dot_general(
        a, b, (((1,), (0,)), ((), ())), preferred_element_type=F32
    )


def knt(a, b):
    return lax.dot_general(
        a, b, (((1,), (1,)), ((), ())), preferred_element_type=F32
    )


def ktn(a, b):
    return lax.dot_general(
        a, b, (((0,), (0,)), ((), ())), preferred_element_type=F32
    )


def low_lanes(shape):
    return lax.broadcasted_iota(jnp.int32, shape, len(shape) - 1) < SPAN


def head_sum(x):
    low = low_lanes(x.shape)
    s0 = jnp.sum(jnp.where(low, x, 0.0), axis=-1, keepdims=True)
    s1 = jnp.sum(jnp.where(low, 0.0, x), axis=-1, keepdims=True)
    return jnp.where(low, s0, s1)


def two_rows(x):
    low = low_lanes(x.shape)
    return jnp.concatenate([jnp.where(low, x, 0.0), jnp.where(low, 0.0, x)], axis=0)


def fold(full):
    return jnp.where(low_lanes((SPAN, 2 * SPAN)), full[:SPAN], full[SPAN:])


def unfold(state):
    low = low_lanes(state.shape)
    return jnp.concatenate([jnp.where(low, state, 0.0), jnp.where(low, 0.0, state)], axis=0)


def running(w, upper=False):
    count = w.shape[0]
    row = lax.broadcasted_iota(jnp.int32, (count, count), 0)
    col = lax.broadcasted_iota(jnp.int32, (count, count), 1)
    keep = (col >= row) if upper else (col <= row)
    return lax.dot_general(
        jnp.where(keep, 1.0, 0.0).astype(F32),
        w,
        (((1,), (0,)), ((), ())),
        precision=HI,
        preferred_element_type=F32,
    )


def strict(count):
    row = lax.broadcasted_iota(jnp.int32, (2 * count, count), 0)
    col = lax.broadcasted_iota(jnp.int32, (2 * count, count), 1)
    row = jnp.where(row >= count, row - count, row)
    return row > col, row == col


def affinity(r, k, u, q, ks):
    count = r.shape[0]
    below, diag = strict(count)
    raw = knt(two_rows(q), ks)
    share = jnp.sum(two_rows(r * u * k), axis=-1, keepdims=True)
    return jnp.where(below, raw, jnp.where(diag, share, 0.0))


def totals_kernel(k_ref, v_ref, w_ref, out_ref):
    cum = running(w_ref[...])
    total = cum[-1:, :]
    kc = k_ref[...] * jnp.exp(total - cum)
    out_ref[0, :SPAN, :] = fold(ktn(v_ref[...], kc))
    out_ref[0, SPAN:, :] = jnp.broadcast_to(jnp.exp(total), (8, 2 * SPAN))


def group_norm(y, gain, bias):
    centred = y - head_sum(y) * (1.0 / SPAN)
    spread = head_sum(centred * centred) * (1.0 / SPAN)
    scale = lax.rsqrt(spread + GN_EPS)
    normal = centred * scale
    return normal, scale, normal * gain + bias


def forward_kernel(r_ref, k_ref, v_ref, w_ref, g_ref, s_ref, p_ref, y_ref, gated_ref):
    r, k, v, w = r_ref[...], k_ref[...], v_ref[...], w_ref[...]
    cum = running(w)
    q = r * jnp.exp(cum - w)
    ks = k * jnp.exp(-cum)
    aff = affinity(r, k, p_ref[0:1, :], q, ks)
    count = r.shape[0]
    v2 = two_rows(v)
    y = (
        knt(q, unfold(s_ref[0]))
        + knn(aff[:count], v2[:count])
        + knn(aff[count:], v2[count:])
    )
    y_ref[...] = y
    gate = g_ref[...]
    _, _, grouped = group_norm(y, p_ref[1:2, :], p_ref[2:3, :])
    gated_ref[...] = (grouped * gate * jax.nn.sigmoid(gate)).astype(BF16)


def gate_kernel(gg_ref, g_ref, y_ref, r_ref, w_ref, p_ref, gate_ref, dy_ref, out_ref):
    gated_grad, gate, y = gg_ref[...], g_ref[...], y_ref[...]
    gain = p_ref[1:2, :]
    normal, scale, grouped = group_norm(y, gain, p_ref[2:3, :])
    sig = jax.nn.sigmoid(gate)
    gate_ref[...] = (gated_grad * grouped * sig * (1.0 + gate * (1.0 - sig))).astype(BF16)
    outer = gated_grad * gate * sig
    inner = outer * gain
    dy = scale * (
        inner
        - head_sum(inner) * (1.0 / SPAN)
        - normal * (head_sum(inner * normal) * (1.0 / SPAN))
    )
    dy_ref[...] = dy
    w = w_ref[...]
    q = r_ref[...] * jnp.exp(running(w) - w)
    out_ref[0, :SPAN, :] = fold(ktn(dy, q))
    gain_grad = jnp.sum(outer * normal, axis=0, keepdims=True)
    bias_grad = jnp.sum(outer, axis=0, keepdims=True)
    out_ref[0, SPAN:, :] = jnp.concatenate(
        [gain_grad, bias_grad, jnp.zeros((6, 2 * SPAN), F32)], axis=0
    )


def backward_kernel(
    r_ref, k_ref, v_ref, w_ref, dy_ref, s_ref, gs_ref, p_ref,
    dr_ref, dk_ref, dv_ref, dd_ref, out_ref,
):
    r, k, v, w, dy = r_ref[...], k_ref[...], v_ref[...], w_ref[...], dy_ref[...]
    u = p_ref[0:1, :]
    count = r.shape[0]
    cum = running(w)
    total = cum[-1:, :]
    e_before, e_minus, e_carry = jnp.exp(cum - w), jnp.exp(-cum), jnp.exp(total - cum)
    q, ks, kc = r * e_before, k * e_minus, k * e_carry
    aff = affinity(r, k, u, q, ks)
    below, _ = strict(count)
    dy2 = two_rows(dy)
    d_aff = jnp.where(below, knt(dy2, v), 0.0)
    own = head_sum(dy * v)
    state, grad_state = s_ref[0], gs_ref[0]
    state2, grad2 = unfold(state), unfold(grad_state)
    ks2 = two_rows(ks)
    dq = knn(dy, state2) + knn(d_aff[:count], ks2[:count]) + knn(d_aff[count:], ks2[count:])
    dks = ktn(d_aff, two_rows(q))
    dkc = knn(v, grad2)
    dv_ref[...] = (ktn(aff, dy2) + knt(kc, grad2)).astype(BF16)
    dr_ref[...] = (dq * e_before + own * u * k).astype(BF16)
    dk_ref[...] = (dks * e_minus + dkc * e_carry + own * u * r).astype(BF16)
    gq, gc = q * dq, kc * dkc
    d_total = jnp.sum(gc, axis=0, keepdims=True) + jnp.exp(total) * jnp.sum(
        state * grad_state, axis=0, keepdims=True
    )
    dw = running(gq - ks * dks - gc, upper=True) - gq + d_total
    term = dw * w
    dd_ref[...] = term.astype(BF16)
    out_ref[0] = jnp.concatenate(
        [
            jnp.sum(term, axis=0, keepdims=True),
            jnp.sum(own * r * k, axis=0, keepdims=True),
            jnp.zeros((6, 2 * SPAN), F32),
        ],
        axis=0,
    )


def block_call(kernel, chunks, step, width, ins, outs, args):
    lane = 2 * SPAN
    kinds = {
        "t": pl.BlockSpec((step, lane), lambda c, h: (c, h)),
        "s": pl.BlockSpec((1, SPAN, lane), lambda c, h: (c, 0, h)),
        "x": pl.BlockSpec((1, SPAN + 8, lane), lambda c, h: (c, 0, h)),
        "e": pl.BlockSpec((1, 8, lane), lambda c, h: (c, 0, h)),
        "p": pl.BlockSpec((8, lane), lambda c, h: (0, h)),
    }
    shapes = {
        "t": lambda d: jax.ShapeDtypeStruct((chunks * step, width), d),
        "x": lambda d: jax.ShapeDtypeStruct((chunks, SPAN + 8, width), d),
        "e": lambda d: jax.ShapeDtypeStruct((chunks, 8, width), d),
    }
    return pl.pallas_call(
        kernel,
        grid=(chunks, width // lane),
        in_specs=[kinds[kind] for kind in ins],
        out_specs=[kinds[kind] for kind, _ in outs],
        out_shape=[shapes[kind](dtype) for kind, dtype in outs],
        compiler_params=pltpu.CompilerParams(vmem_limit_bytes=48 * 1024 * 1024),
    )(*args)


def weight_grad(places, pairs, block):
    tokens, blocks = pairs[0][0].shape[0], places.shape[0]
    widths = [y.shape[1] for _, y in pairs]

    def kernel(_, *refs):
        at = 0
        for i, wide in enumerate(widths):
            refs[-1][0, :, at : at + wide] = tn(refs[2 * i][...], refs[2 * i + 1][...]).astype(
                BF16
            )
            at += wide

    specs = []
    for wide in widths:
        specs.append(pl.BlockSpec((tokens, block), lambda i, at: (0, at[i])))
        specs.append(pl.BlockSpec((tokens, wide), lambda i, at: (0, 0)))
    return pl.pallas_call(
        kernel,
        grid_spec=pltpu.PrefetchScalarGridSpec(
            num_scalar_prefetch=1,
            grid=(blocks,),
            in_specs=specs,
            out_specs=pl.BlockSpec((1, block, sum(widths)), lambda i, at: (i, 0, 0)),
        ),
        out_shape=jax.ShapeDtypeStruct((blocks, block, sum(widths)), BF16),
        compiler_params=pltpu.CompilerParams(vmem_limit_bytes=48 * 1024 * 1024),
    )(places, *[v for pair in pairs for v in pair])


def lanes_kernel(spans, x_ref, out_ref):
    at = 0
    for start, stop in spans:
        out_ref[:, at : at + stop - start] = x_ref[:, start:stop].astype(out_ref.dtype)
        at += stop - start


def move_lanes(spans, value, dtype):
    return pl.pallas_call(
        functools.partial(lanes_kernel, spans),
        in_specs=[pl.BlockSpec(memory_space=pltpu.VMEM)],
        out_specs=pl.BlockSpec(memory_space=pltpu.VMEM),
        out_shape=jax.ShapeDtypeStruct(value.shape, dtype),
        compiler_params=pltpu.CompilerParams(vmem_limit_bytes=32 * 1024 * 1024),
    )(value)


def place_kernel(counts, wide, block, at_ref, *refs):
    ins, out_ref, sems = refs[: len(counts)], refs[-2], refs[-1]
    rows = out_ref.shape[0]
    copies, i = [], 0
    for ref, n in zip(ins, counts):
        for j in range(n):
            start = pl.multiple_of(at_ref[i] * block, block)
            column = i * block // rows * wide
            copy = pltpu.make_async_copy(
                ref.at[pl.ds(j * block, block), :],
                out_ref.at[pl.ds(start, block), pl.ds(column, wide)],
                sems.at[i],
            )
            copy.start()
            copies.append(copy)
            i += 1
    for copy in copies:
        copy.wait()


def place_rows(parts, block):
    pieces = [p for part in parts for p in part[1]]
    wide = pieces[0].shape[1]
    at = jnp.concatenate([part[0] for part in parts])
    counts = [p.shape[0] // block for p in pieces]
    total = sum(counts)
    return pl.pallas_call(
        functools.partial(place_kernel, counts, wide, block),
        in_specs=[pl.BlockSpec(memory_space=pltpu.SMEM)]
        + [pl.BlockSpec(memory_space=pl.ANY)] * len(pieces),
        out_specs=pl.BlockSpec(memory_space=pl.ANY),
        out_shape=jax.ShapeDtypeStruct(
            (total * block // len(parts), wide * len(parts)), pieces[0].dtype
        ),
        scratch_shapes=[pltpu.SemaphoreType.DMA((total,))],
        compiler_params=pltpu.CompilerParams(vmem_limit_bytes=32 * 1024 * 1024),
    )(at, *pieces)


def mixes_kernel(
    open_ref, x_ref, before_ref, vec_ref, down_ref, up_ref, ddown_ref,
    m1_ref, m2_ref, m3_ref, m4_ref, dh_ref,
    normal_ref, scale_ref, delta_ref, blend_ref, m0_ref, tanh_ref, dtanh_ref,
):
    piece = pl.program_id(0)
    step = m1_ref.shape[0]
    x = x_ref[...].astype(F32)
    centred = x - jnp.mean(x, axis=-1, keepdims=True)
    scale = lax.rsqrt(jnp.mean(centred * centred, axis=-1, keepdims=True) + LN_EPS)
    normal = centred * scale
    full = normal * vec_ref[0:1, :] + vec_ref[1:2, :]
    normed = full[:step]
    first = jnp.where(open_ref[piece] == 1, before_ref[0:1, :], full[step : step + 1])
    row = lax.broadcasted_iota(jnp.int32, normed.shape, 0)
    delta = jnp.where(row == 0, first, pltpu.roll(normed, 1, 0)) - normed
    blend = (normed + delta * vec_ref[2:3, :]).astype(BF16)
    tanh = jnp.tanh(nn(blend, down_ref[...]))
    latent = tanh.astype(BF16)
    lane = lax.broadcasted_iota(jnp.int32, latent.shape, 1)
    mixed = []
    for c in range(5):
        own = (lane >= c * RANK) & (lane < (c + 1) * RANK)
        offset = nt(jnp.where(own, latent, jnp.zeros_like(latent)), up_ref[...])
        mixed.append((normed + delta * (vec_ref[3 + c : 4 + c, :] + offset)).astype(BF16))
    dtanh = jnp.tanh(nn(mixed[0], ddown_ref[...]))
    m1_ref[...], m2_ref[...], m3_ref[...], m4_ref[...] = mixed[1:]
    dh_ref[...] = dtanh.astype(BF16)

    @pl.when(piece == 0)
    def _():
        normal_ref[...] = normal[:step]
        scale_ref[...] = jnp.broadcast_to(scale[:step], scale_ref.shape)
        delta_ref[...] = delta
        blend_ref[...] = blend
        m0_ref[...] = mixed[0]
        tanh_ref[...] = tanh
        dtanh_ref[...] = dtanh


def group_mixes(opening, x, before, vec, down, up, ddown, step):
    high, width = step + 16, x.shape[1]
    pieces = x.shape[0] // high

    def whole(value):
        return pl.BlockSpec(value.shape, lambda k: (0, 0))

    def own(columns, dtype):
        return (
            pl.BlockSpec((step, columns), lambda k: (0, 0)),
            jax.ShapeDtypeStruct((step, columns), dtype),
        )

    def every(columns, dtype):
        return (
            pl.BlockSpec((step, columns), lambda k: ((k % 2) * 2 + k // 2, 0)),
            jax.ShapeDtypeStruct((pieces * step, columns), dtype),
        )

    outs = [every(width, BF16)] * 4 + [
        every(DRANK, BF16),
        own(width, F32),
        own(128, F32),
        own(width, F32),
        own(width, BF16),
        own(width, BF16),
        own(5 * RANK, F32),
        own(DRANK, F32),
    ]
    return pl.pallas_call(
        mixes_kernel,
        grid=(pieces,),
        in_specs=[
            pl.BlockSpec(memory_space=pltpu.SMEM),
            pl.BlockSpec((high, width), lambda k: (k, 0)),
            whole(before),
            whole(vec),
            whole(down),
            whole(up),
            whole(ddown),
        ],
        out_specs=[o[0] for o in outs],
        out_shape=[o[1] for o in outs],
        compiler_params=pltpu.CompilerParams(vmem_limit_bytes=56 * 1024 * 1024),
    )(opening, x, before, vec, down, up, ddown)


def product(pairs, outs, body, sides=(), tile=256):
    count = len(pairs)

    def kernel(*refs):
        ins, out_refs = refs[: 2 * count + len(sides)], refs[2 * count + len(sides) :]
        products = [
            (nn if pair[2] == "nn" else nt)(ins[2 * i][...], ins[2 * i + 1][...])
            for i, pair in enumerate(pairs)
        ]
        results = body(*products, *[r[...] for r in ins[2 * count :]])
        for ref, value in zip(out_refs, results):
            ref[...] = value.astype(ref.dtype)

    specs, args = [], []
    for a, b, form, at in pairs:
        depth = a.shape[1]
        specs.append(pl.BlockSpec(a.shape, lambda j: (0, 0)))
        if form == "nn":
            specs.append(pl.BlockSpec((depth, tile), lambda j, at=at: (0, at + j)))
        else:
            specs.append(pl.BlockSpec((tile, depth), lambda j, at=at: (j, at)))
        args += [a, b]
    for side in sides:
        specs.append(pl.BlockSpec((side.shape[0], tile), lambda j: (0, j)))
    return pl.pallas_call(
        kernel,
        grid=(outs[0][1] // tile,),
        in_specs=specs,
        out_specs=[pl.BlockSpec((o[0], tile), lambda j: (0, j)) for o in outs],
        out_shape=[jax.ShapeDtypeStruct(o[:2], o[2]) for o in outs],
        compiler_params=pltpu.CompilerParams(vmem_limit_bytes=56 * 1024 * 1024),
    )(*args, *sides)


def local(fn, outs, *args, scalar=None):
    def kernel(*refs):
        lead = [] if scalar is None else [refs[0]]
        ins, out_refs = refs[len(lead) : -len(outs)], refs[-len(outs) :]
        scalars = [r[i] for r in lead for i in range(r.shape[0])]
        results = fn(*scalars, *[r[...] for r in ins])
        for ref, value in zip(out_refs, results):
            ref[...] = value.astype(ref.dtype)

    specs = [pl.BlockSpec(memory_space=pltpu.VMEM)] * len(args)
    if scalar is not None:
        specs = [pl.BlockSpec(memory_space=pltpu.SMEM)] + specs
        args = (scalar.reshape(-1), *args)
    return pl.pallas_call(
        kernel,
        in_specs=specs,
        out_specs=[pl.BlockSpec(memory_space=pltpu.VMEM)] * len(outs),
        out_shape=[jax.ShapeDtypeStruct(o[:2], o[2]) for o in outs],
        compiler_params=pltpu.CompilerParams(vmem_limit_bytes=56 * 1024 * 1024),
    )(*args)


def take_lanes(value, spans):
    if len(spans) == 1:
        return value
    return jnp.concatenate([value[:, a:b] for a, b in spans], axis=1)


def norm_back(grad, gain, normal, scale):
    e = grad * gain
    return scale * (
        e
        - jnp.mean(e, axis=-1, keepdims=True)
        - normal * jnp.mean(e * normal, axis=-1, keepdims=True)
    )


def rows_above(value, first):
    row = lax.broadcasted_iota(jnp.int32, value.shape, 0)
    return jnp.where(row == 0, first, pltpu.roll(value, 1, 0))


def rows_below(value, last):
    row = lax.broadcasted_iota(jnp.int32, value.shape, 0)
    high = value.shape[0]
    return jnp.where(row == high - 1, last, pltpu.roll(value, high - 1, 0))


def padded(rows):
    return jnp.concatenate(
        list(rows) + [jnp.zeros((8 - len(rows), rows[0].shape[1]), F32)], axis=0
    )


def column_sum(value):
    return jnp.sum(value, axis=0, keepdims=True)


def gates_kernel(
    spans, who_ref, middle_ref, value_ref, more_ref, act_ref, cot_ref,
    out_ref, up_ref, vg_ref, rg_ref, held,
):
    to_spans, from_spans = spans
    step, part = act_ref.shape[0] // 4, act_ref.shape[1]
    who = who_ref[0]
    act = [
        act_ref[pl.ds(pl.multiple_of((who ^ j) * step, step), step), :] for j in range(4)
    ]
    recept = jax.nn.sigmoid(take_lanes(jnp.concatenate(act, axis=1).astype(F32), to_spans))
    value = value_ref[...] + more_ref[...].astype(F32)
    out = middle_ref[...] + recept * value
    out_ref[...] = take_lanes(out, from_spans).astype(BF16)
    up = take_lanes(cot_ref[...].astype(F32), to_spans)
    up_ref[...] = up
    vg_ref[...] = (up * recept).astype(BF16)
    held[...] = take_lanes(up * value * recept * (1.0 - recept), from_spans)
    for k in range(4):
        at = pl.multiple_of((who ^ k) * part, part)
        rg_ref[k * step : (k + 1) * step, :] = held[:, pl.ds(at, part)].astype(BF16)


def gates(spans, who, middle, value, more, act, cot):
    step, width = middle.shape
    part = act.shape[1]
    shape = jax.ShapeDtypeStruct
    return pl.pallas_call(
        functools.partial(gates_kernel, spans),
        in_specs=[pl.BlockSpec(memory_space=pltpu.SMEM)]
        + [pl.BlockSpec(memory_space=pltpu.VMEM)] * 5,
        out_specs=[pl.BlockSpec(memory_space=pltpu.VMEM)] * 4,
        out_shape=[
            shape((step, width), BF16),
            shape((step, width), F32),
            shape((step, width), BF16),
            shape((4 * step, part), BF16),
        ],
        scratch_shapes=[pltpu.VMEM((step, width), F32)],
        compiler_params=pltpu.CompilerParams(vmem_limit_bytes=56 * 1024 * 1024),
    )(who.reshape(1), middle, value, more, act, cot)


def mixes_back_kernel(
    kept_ref, got_ref, dl_ref, dl_more_ref, delta_ref, tanh_ref, dtanh_ref, blend_ref, m0_ref,
    down_ref, up_ref, ddown_ref, vec_ref,
    rest_ref, dg_ref, row_ref, cols_ref, down_out, up_out, ddown_out,
):
    step = delta_ref.shape[0]
    dtanh = dtanh_ref[...]
    decay_grad = dl_ref[...] + dl_more_ref[...].astype(F32)
    decay_pre = (decay_grad * (1.0 - dtanh * dtanh)).astype(BF16)
    ddown_out[...] = tn(m0_ref[...], decay_pre)
    tanh = tanh_ref[...]
    latent = tanh.astype(BF16)
    lane = lax.broadcasted_iota(jnp.int32, latent.shape, 1)
    delta, up = delta_ref[...], up_ref[...]
    latent_grad = jnp.zeros(latent.shape, F32)
    up_grad = jnp.zeros(up_out.shape, F32)
    dg = jnp.zeros(delta.shape, F32)
    total = jnp.zeros(delta.shape, F32)
    cols = []
    for c in range(5):
        own = (lane >= c * RANK) & (lane < (c + 1) * RANK)
        mine = jnp.where(own, latent, jnp.zeros_like(latent))
        if c == 0:
            grad = nt(decay_pre, ddown_ref[...])
        else:
            at = slice((c - 1) * step, c * step)
            grad = kept_ref[at, :] + got_ref[at, :].astype(F32)
        shift = grad * delta
        cols.append(column_sum(shift))
        offset = shift.astype(BF16)
        latent_grad = jnp.where(own, nn(offset, up), latent_grad)
        up_grad = up_grad + tn(offset, mine)
        dg = dg + grad * (vec_ref[3 + c : 4 + c, :] + nt(mine, up))
        total = total + grad
    up_out[...] = up_grad
    mix_pre = (latent_grad * (1.0 - tanh * tanh)).astype(BF16)
    down_out[...] = tn(blend_ref[...], mix_pre)
    blend_grad = nt(mix_pre, down_ref[...])
    dg = dg + blend_grad * vec_ref[2:3, :]
    rest_ref[...] = total + blend_grad - dg
    dg_ref[...] = dg
    row_ref[...] = dg[:8]
    cols_ref[...] = padded([column_sum(blend_grad * delta)] + cols)


def mixes_back(*args):
    delta, down, ddown = args[4], args[9], args[11]
    step, width = delta.shape
    shape = jax.ShapeDtypeStruct
    outs = [
        shape((step, width), F32),
        shape((step, width), F32),
        shape((8, width), F32),
        shape((8, width), F32),
        shape(down.shape, F32),
        shape(down.shape, F32),
        shape(ddown.shape, F32),
    ]
    return pl.pallas_call(
        mixes_back_kernel,
        in_specs=[pl.BlockSpec(memory_space=pltpu.VMEM)] * len(args),
        out_specs=[pl.BlockSpec(memory_space=pltpu.VMEM)] * len(outs),
        out_shape=outs,
        compiler_params=pltpu.CompilerParams(vmem_limit_bytes=60 * 1024 * 1024),
    )(*args)


def tie(*values):
    return lax.optimization_barrier(values)


def on_device(
    count,
    tokens,
    previous,
    initial_state,
    mixing_weights,
    lowrank_weights,
    vectors,
    feedforward_weights,
    cotangent,
):
    fast = initial_state.shape[0] == 64
    masks = (1, 8) if fast else (1, 2)
    size = 1 << len(masks)
    teams = count // size
    all_masks = [1 << b for b in range(count.bit_length() - 1)]
    team_masks = [b for b in all_masks if b not in masks]
    far = 16
    team_masks.sort(key=lambda b: fast and b != far)
    me = lax.axis_index("seq")
    _, step, width = tokens.shape
    rows = mixing_weights.shape[0]
    part = width // size
    ff_part = FF // size
    team_rows = rows * size
    def bit_of(who, mask):
        return (who // mask) % 2 if isinstance(who, int) else lax.rem(lax.div(who, mask), 2)

    def member_of(who):
        return sum(bit_of(who, b) << j for j, b in enumerate(masks))

    def team_of(who):
        return sum(bit_of(who, b) << j for j, b in enumerate(team_masks))

    member, team = member_of(me), team_of(me)
    order = sorted(range(count), key=lambda d: (team_of(d), member_of(d)))
    inverse = sorted(range(count), key=lambda p: order[p])
    across = [order[m::size] for m in range(size)]
    square = [order[m :: 2 * size] for m in range(2 * size)]
    def lane_spans(blocks):
        spans = []
        for d in blocks:
            if spans and spans[-1][1] == d * rows:
                spans[-1][1] = (d + 1) * rows
            else:
                spans.append([d * rows, (d + 1) * rows])
        return spans

    to_spans, from_spans = lane_spans(order), lane_spans(inverse)

    def to_places(value, dtype):
        return move_lanes(to_spans, value, dtype)

    def flips(k):
        return sum(b for j, b in enumerate(masks) if (k >> j) & 1)

    def trade(value, mask):
        return lax.ppermute(value, "seq", [(d, d ^ mask) for d in range(count)])

    def group_gather(value):
        side = trade(value, masks[1])
        return value, side, trade(jnp.concatenate([value, side], axis=0), masks[0])

    def group_rows(value):
        high, columns = value.shape

        def lay(own, side, far):
            return (jnp.concatenate([own, far[:high], side, far[high:]], axis=0),)

        return local(lay, [(size * high, columns, value.dtype)], *group_gather(value))[0]

    def halves(value):
        cut = [value[k * step : (k + 1) * step] for k in range(size)]
        return [cut[0], cut[2]], [cut[1], cut[3]]

    def group_fold(kept, sent):
        high, columns = kept.shape[0] // 2, kept.shape[1]
        got = trade(sent, masks[0])

        def add(mine, more):
            total = mine + more.astype(F32)
            return total[:high], total[high:]

        return local(add, [(high, columns, F32), (high, columns, BF16)], kept, got)

    def group_sum(kept, sent):
        mine, side = group_fold(kept, sent)
        return mine, trade(side, masks[1])

    def crossing_sum(*pairs):
        units = len(pairs)

        def body(*products):
            parts = [halves(p) for p in products]
            kept = [p[0][i] for i in range(2) for p in parts]
            sent = [p[1][i] for i in range(2) for p in parts]
            return jnp.concatenate(kept, axis=0), jnp.concatenate(sent, axis=0)

        high = 2 * units * step
        return product(
            [(a, b, "nt", at) for a, b, at in pairs],
            [(high, width, F32), (high, width, BF16)],
            body,
            tile=512,
        )

    def exchange(pieces):
        pieces, high = list(pieces), pieces[0].shape[0]
        for j in reversed(range(len(masks))):
            keys = [k for k in range(size) if (k >> j) & 1]
            got = trade(jnp.concatenate([pieces[k] for k in keys], axis=0), masks[j])
            for i, k in enumerate(keys):
                pieces[k] = got[i * high : (i + 1) * high]
        return pieces

    def ordered(pieces):
        pieces = list(pieces)
        for j in range(len(masks)):
            swap = lax.rem(lax.div(member, 1 << j), 2) == 1
            pieces = [
                jnp.where(swap, pieces[k ^ (1 << j)], pieces[k]) for k in range(len(pieces))
            ]
        return pieces

    def neighbour(value, offset):
        pairs = [(d, d + offset) for d in range(count) if 0 <= d + offset < count]
        return lax.ppermute(value, "seq", pairs)

    def take_columns(value, spans, who):
        return jnp.concatenate(
            [
                lax.dynamic_slice_in_dim(value, start + who * wide, wide, axis=1)
                for start, wide in spans
            ],
            axis=1,
        )

    def group_columns(value, spans):
        pieces = [take_columns(value, spans, member ^ k) for k in range(size)]
        return jnp.concatenate(ordered(exchange(pieces)), axis=0)

    def crossing(first):
        bits = list(range(1, len(team_masks))) + [0]
        if first:
            bits[0], bits[1] = bits[1], bits[0]
        return bits

    def gather_rows(own):
        return lax.all_gather(own, "seq", axis=0, tiled=True, axis_index_groups=across)

    def far_send(own):
        return trade(own, far) if fast else own

    def far_join(own, got):
        if not fast:
            return own
        upper = bit_of(me, far) == 1
        return jnp.concatenate(
            [jnp.where(upper, got, own), jnp.where(upper, own, got)], axis=0
        )

    def gather_square(paired):
        groups = square if fast else across
        return lax.all_gather(paired, "seq", axis=0, tiled=True, axis_index_groups=groups)

    def team_products(*pairs):
        if fast:
            places = jnp.arange(teams, dtype=jnp.int32)
            return weight_grad(places, pairs, team_rows).reshape(width, -1)
        return jnp.concatenate([tn(x, y).astype(BF16) for x, y in pairs], axis=1)

    def square_sum(grads):
        groups = square if fast else across
        return lax.psum_scatter(
            grads, "seq", scatter_dimension=0, tiled=True, axis_index_groups=groups
        )

    def far_split(pair):
        if not fast:
            return pair, jnp.zeros_like(pair)
        bit = bit_of(me, far)
        sent = lax.dynamic_slice_in_dim(pair, (1 - bit) * team_rows, team_rows, axis=0)
        kept = lax.dynamic_slice_in_dim(pair, bit * team_rows, team_rows, axis=0)
        return kept, trade(sent, far)

    def far_add(kept, got):
        return (kept.astype(F32) + got.astype(F32)).astype(BF16)

    def cube_gather(value, follower=None):
        for mask in reversed(all_masks):
            got = trade(value, mask)
            upper = bit_of(me, mask) == 1
            value = jnp.stack([jnp.where(upper, got, value), jnp.where(upper, value, got)])
            if mask == 8 and follower is not None:
                value, follower = tie(value, follower)
        axes = len(all_masks)
        cube = value.transpose(*reversed(range(axes)), *range(axes, value.ndim))
        return cube if follower is None else (cube, follower)

    place_axes = [all_masks[::-1].index(b) for b in team_masks[::-1] + list(masks[::-1])]

    def by_place(cube):
        rest = range(len(all_masks), cube.ndim)
        return cube.transpose(*place_axes, *rest).reshape(width, -1)

    def to_cube(value):
        cube = value.reshape(*[2] * len(place_axes), rows, -1)
        back = [place_axes.index(a) for a in range(len(place_axes))]
        return cube.transpose(*back, len(back), len(back) + 1)

    def cube_sum(cube, kind, follower):
        for axis, mask in reversed(list(enumerate(reversed(all_masks)))):
            bit = bit_of(me, mask)
            sent = lax.dynamic_index_in_dim(cube, 1 - bit, axis, keepdims=False)
            kept = lax.dynamic_index_in_dim(cube, bit, axis, keepdims=False)
            cube = kept.astype(F32) + trade(sent.astype(kind), mask).astype(F32)
            if mask == 2:
                cube, follower = tie(cube, follower)
        return cube, follower

    def hand_rows(pieces, extra=None):
        widths = [sum(p.shape[1] for p in piece) for piece in pieces]
        joint = jnp.concatenate([p for piece in pieces for p in piece], axis=1)
        mine = [
            lax.dynamic_slice_in_dim(joint, (member ^ k) * rows, rows, axis=0)
            for k in range(size)
        ]
        if extra is not None:
            mine = [jnp.concatenate([m, e], axis=1) for m, e in zip(mine, extra)]
        by_place = exchange(mine)
        by_member = ordered(by_place)
        outs, start = [], 0
        for wide in widths:
            outs += [p[:, start : start + wide] for p in by_member]
            start += wide
        joined = jnp.concatenate(outs, axis=1).astype(F32)
        if extra is None:
            return joined
        return joined, [p[:, start:].astype(F32) for p in by_place]

    up_start, decay_start, decay_up = 5 * RANK, 10 * RANK, 10 * RANK + DRANK
    last_row = neighbour(tokens[0, -1:, :], 1)
    tokens_sent = to_places(
        jnp.concatenate([tokens[0], jnp.broadcast_to(last_row, (16, width))], axis=0), BF16
    )
    natural, mix_in = cube_gather(
        jnp.concatenate(
            [vectors, initial_state, lowrank_weights[:, decay_up:].astype(F32)], axis=1
        ),
        mixing_weights,
    )
    natural = natural.reshape(width, -1)
    low_cube, mix_in = cube_gather(lowrank_weights[:, :decay_up], mix_in)
    tokens_all = jnp.concatenate(group_gather(tokens_sent), axis=0)
    mix_local = group_columns(mix_in, [(c * width, part) for c in range(5)])
    mix_local, natural, low_cube, tokens_all = tie(mix_local, natural, low_cube, tokens_all)
    lowrank = by_place(low_cube)
    mix_kv, mix_rest = mix_local[:, : 2 * part], mix_local[:, 2 * part :]
    kv_got, mix_rest, feed_in = tie(far_send(mix_kv), mix_rest, feedforward_weights)
    w_kv = gather_square(far_join(mix_kv, kv_got))
    tiles = part // 256

    mine = lax.dynamic_slice_in_dim(natural, member * part, part, axis=0)
    vec_part = mine[:, :16].T
    first_state = mine[:, 16 : 16 + SPAN].T
    w_dup = mine[:, 16 + SPAN :].astype(BF16)
    vec = by_place(
        natural[:, :16].reshape(*[2] * len(all_masks), rows, 16)
    ).T
    wkv_rows = jnp.concatenate([vec_part[9:12], jnp.zeros((5, part), F32)], axis=0)
    is_first = (me == 0).astype(jnp.int32)
    before = to_places(previous.reshape(2, width), F32)
    w_down, w_up = lowrank[:, :up_start], lowrank[:, up_start:decay_start]
    w_ddown = lowrank[:, decay_start:]

    opening = jnp.stack(
        [jnp.bitwise_xor(me, flips(k)) == 0 for k in (0, 2, 1, 3)]
    ).astype(jnp.int32)
    (
        *mixed_all, dh_all, normal_one, scale_one, delta, blend, mixed_zero, mix_tanh, decay_tanh,
    ) = group_mixes(opening, tokens_all, before, vec, w_down, w_up, w_ddown, step)
    rest_got, mixed_all[0] = tie(far_send(mix_rest), mixed_all[0])
    w_rest = gather_square(far_join(mix_rest, rest_got))
    ff_spans = [(0, ff_part), (FF, part), (FF + width, ff_part)]
    ff_local = group_columns(feed_in, ff_spans)
    everyone = size * step
    (log_decay,) = product(
        [(dh_all, w_dup, "nt", 0)],
        [(everyone, part, F32)],
        lambda acc, base: (-jnp.exp(base + acc),),
        sides=(vec_part[8:9],),
    )
    keys, values = product(
        [(mixed_all[0], w_kv, "nn", 0), (mixed_all[1], w_kv, "nn", tiles)],
        [(everyone, part, F32)] * 2,
        lambda a, b: (a, b),
    )

    keys, ff_local = tie(keys, ff_local)
    ff_tail = ff_local[:, ff_part + part :]
    ff_near = ff_local[:, : ff_part + part]
    near_got = far_send(ff_near)

    call = functools.partial(block_call, chunks=size, step=step, width=part)
    (totals,) = call(
        totals_kernel, ins="ttt", outs=[("x", F32)], args=(keys, values, log_decay)
    )
    stages, current = [], [None, []]
    for mask in all_masks:
        if mask in masks:
            current[1].append(1 << masks.index(mask))
        else:
            stages.append(current)
            current = [mask, []]
    stages.append(current)
    high, long = SPAN + 8, SPAN + 16

    def chain(early, late):
        return early[0] * late[0], late[0] * early[1] + late[1]

    def pick(flag, yes, no):
        return tuple(jnp.where(flag, a, b) for a, b in zip(yes, no))

    def rows8(row):
        return jnp.broadcast_to(row, (8, part))

    def pack(items):
        return jnp.concatenate([r for d, v in items for r in (v, rows8(d))], axis=0)

    def unpack(array, count):
        cut = [array[i * high : (i + 1) * high] for i in range(count)]
        return [(c[SPAN : SPAN + 1], c[:SPAN]) for c in cut]

    def swap_members(who, pieces):
        pieces = list(pieces)
        for j in range(len(masks)):
            flag = (who // (1 << j)) % 2 == 1
            pieces = [jnp.where(flag, pieces[k ^ (1 << j)], pieces[k]) for k in range(size)]
        return pieces

    def neutral():
        return jnp.ones((1, part), F32), jnp.zeros((SPAN, part), F32)

    def flags_of(mask):
        bit = jnp.int32(0) if mask is None else bit_of(me, mask)
        return jnp.stack([member, bit]).astype(jnp.int32)

    keys_at, decays = list(range(size)), []
    open_bits = size - 1
    stage_arrays = [totals.reshape(size * high, part)]
    for index, (mask, merges) in enumerate(stages):
        last = index + 1 == len(stages)
        after_keys = keys_at
        for bit in merges:
            after_keys = [g for g in after_keys if not g & bit]

        def forward_stage(
            who, late, *arrays, mask=mask, merges=merges, groups=keys_at, bits=open_bits, last=last
        ):
            marks = []
            if mask is None:
                cut = [arrays[0][k * high : (k + 1) * high] for k in range(size)]
                total = {
                    m: (p[SPAN : SPAN + 1], p[:SPAN])
                    for m, p in enumerate(swap_members(who, cut))
                }
                chunks = [neutral() for _ in range(size)]
            else:
                total = dict(zip(groups, unpack(arrays[0], len(groups))))
                chunks = unpack(arrays[1], size)
                other = {}
                for i, g in enumerate(groups):
                    got = arrays[2][i * long : (i + 1) * long].astype(F32)
                    other[g] = got[SPAN : SPAN + 1] + got[SPAN + 8 : SPAN + 9], got[:SPAN]
                marks += [total[g][0] for g in groups] + [other[g][0] for g in groups]
                late = late == 1
                chunks = [
                    pick(late, chain(other[m & bits], c), c) for m, c in enumerate(chunks)
                ]
                total = {
                    g: pick(late, chain(other[g], total[g]), chain(total[g], other[g]))
                    for g in groups
                }
            for bit in merges:
                marks += [total[g][0] for g in total]
                chunks = [
                    chain(total[(m & bits) ^ bit], c) if m & bit else c
                    for m, c in enumerate(chunks)
                ]
                total = {g: chain(total[g], total[g | bit]) for g in total if not g & bit}
                bits ^= bit
            marks = jnp.concatenate([rows8(r) for r in marks], axis=0)
            if last:
                states = [d * arrays[-1] + v for d, v in chunks]
                return jnp.concatenate(swap_members(who, states), axis=0), marks
            sent = []
            for d, v in total.values():
                first = d.astype(BF16)
                rest = (d - first.astype(F32)).astype(BF16)
                sent += [v.astype(BF16), rows8(first), rows8(rest)]
            return (
                pack(list(total.values())), pack(chunks), jnp.concatenate(sent, axis=0), marks
            )

        count_marks = (0 if mask is None else 2 * len(keys_at)) + sum(
            len(keys_at) >> i for i in range(len(merges))
        )
        marks_out = (8 * count_marks, part, F32)
        if last:
            outs = [(size * SPAN, part, F32), marks_out]
            state_in, marks = local(
                forward_stage, outs, *stage_arrays, first_state, scalar=flags_of(mask)
            )
            state_in = state_in.reshape(size, SPAN, part)
        else:
            outs = [
                (len(after_keys) * high, part, F32),
                (size * high, part, F32),
                (len(after_keys) * long, part, BF16),
                marks_out,
            ]
            total, chunks, sent, marks = local(
                forward_stage, outs, *stage_arrays, scalar=flags_of(mask)
            )
            if mask == (2 if fast else 4):
                sent, near_got = tie(sent, near_got)
            stage_arrays = [total, chunks, trade(sent, stages[index + 1][0])]
        decays.append(marks)
        keys_at = after_keys
        for bit in merges:
            open_bits ^= bit
    w_near = gather_square(far_join(ff_near, near_got))
    w_key, w_rec = w_near, w_near[:, ff_part:]
    state_in, ff_tail = tie(state_in, ff_tail)
    val_got = far_send(ff_tail)

    receipt, gate_pre = product(
        [(mixed_all[2], w_rest, "nn", 0), (mixed_all[3], w_rest, "nn", tiles)],
        [(everyone, part, F32)] * 2,
        lambda a, b: (a, b),
    )
    wkv, gated = call(
        forward_kernel,
        ins="tttttsp",
        outs=[("t", F32), ("t", BF16)],
        args=(receipt, keys, values, log_decay, gate_pre, state_in, wkv_rows),
    )
    gated, val_got = tie(gated, val_got)
    w_val = gather_square(far_join(ff_tail, val_got))
    branch, branch_more = group_sum(*crossing_sum((gated, w_rest, 2)))

    def norm_two(hidden, mine, more, vec):
        middle = hidden[:step].astype(F32) + mine + more.astype(F32)
        centred = middle - jnp.mean(middle, axis=-1, keepdims=True)
        scale = lax.rsqrt(jnp.mean(centred * centred, axis=-1, keepdims=True) + LN_EPS)
        normal = centred * scale
        tail = normal[step - 8 :] * vec[12:13] + vec[13:14]
        return middle, normal, jnp.broadcast_to(scale, (step, 128)), tail

    whole = (step, width, F32)
    middle, normal_two, scale_two, tail_two = local(
        norm_two,
        [whole, whole, (step, 128, F32), (8, width, F32)],
        tokens_sent,
        branch,
        branch_more,
        vec,
    )

    def mix_two(first, normal, arrived, before, vec):
        normed = normal * vec[12:13] + vec[13:14]
        above = jnp.where(first == 1, before[1:2], arrived[7:8])
        delta = rows_above(normed, above) - normed
        key_in, recv_in = normed + delta * vec[14:15], normed + delta * vec[15:16]
        return jnp.concatenate([key_in, recv_in], axis=0), delta

    both, delta_two = local(
        mix_two,
        [(2 * step, width, BF16), whole],
        normal_two,
        neighbour(tail_two, 1),
        before,
        vec,
        scalar=is_first,
    )

    key_all, recv_all = group_rows(both[:step]), group_rows(both[step:])
    relu, squared = product(
        [(key_all, w_key, "nn", 0)],
        [(everyone, ff_part, F32), (everyone, ff_part, BF16)],
        lambda acc: (jnp.maximum(acc, 0.0), jnp.square(jnp.maximum(acc, 0.0))),
        tile=ff_part // 2,
    )
    (recept_act,) = product(
        [(recv_all, w_rec, "nn", 0)],
        [(everyone, part, BF16)],
        lambda acc: (acc,),
    )
    squared, recept_act = tie(squared, recept_act)
    acts = exchange([recept_act[k * step : (k + 1) * step] for k in range(size)])
    value, value_more = group_sum(*crossing_sum((squared, w_val, 0)))
    block_output, upstream, value_grad, recept_grads = gates(
        (to_spans, from_spans),
        member,
        middle,
        value,
        value_more,
        jnp.concatenate(acts, axis=0),
        cotangent.reshape(step, width),
    )

    rg_all = jnp.concatenate(
        exchange([recept_grads[k * step : (k + 1) * step] for k in range(size)]), axis=0
    )
    vg_all = group_rows(value_grad)
    val_grads = team_products((vg_all, squared))
    vg_all, val_grads, rg_all = tie(vg_all, val_grads, rg_all)
    val_pair = square_sum(val_grads)
    (key_grad,) = product(
        [(vg_all, w_val, "nn", 0)],
        [(everyone, ff_part, BF16)],
        lambda acc, relu: (acc * (2.0 * relu),),
        sides=(relu,),
        tile=ff_part // 2,
    )
    key_grads = team_products((key_all, key_grad))
    key_grad, key_grads = tie(key_grad, key_grads)
    key_pair = square_sum(key_grads)
    recv_two = group_sum(*crossing_sum((rg_all, w_rec, 0)))
    key_two = group_sum(*crossing_sum((key_grad, w_key, 0)))

    def inputs_back(key, key_more, recv, recv_more, vec):
        key, recv = key + key_more.astype(F32), recv + recv_more.astype(F32)
        top = key[:8] * vec[14:15] + recv[:8] * vec[15:16]
        return jnp.concatenate([key, recv], axis=0), top

    in_grads, top_two = local(
        inputs_back, [(2 * step, width, F32), (8, width, F32)], *key_two, *recv_two, vec
    )
    last_flag = (me == count - 1).astype(jnp.int32)

    def norm_two_back(last, grads, arrived, upstream, normal, scale, delta, vec):
        key_grad, recv_grad = grads[:step], grads[step:]
        shifted = key_grad * vec[14:15] + recv_grad * vec[15:16]
        below = jnp.where(last == 1, jnp.zeros_like(arrived[:1]), arrived[:1])
        grad = (
            key_grad * (1.0 - vec[14:15])
            + recv_grad * (1.0 - vec[15:16])
            + rows_below(shifted, below)
        )
        out = upstream + norm_back(grad, vec[12:13], normal, scale[:, :1])
        cols = padded(
            [
                column_sum(grad * normal),
                column_sum(grad),
                column_sum(key_grad * delta),
                column_sum(recv_grad * delta),
            ]
        )
        return out, out, cols

    middle_grad, branch_grad, cols_two = local(
        norm_two_back,
        [whole, (step, width, BF16), (8, width, F32)],
        in_grads,
        neighbour(top_two, -1),
        upstream,
        normal_two,
        scale_two,
        delta_two,
        vec,
        scalar=last_flag,
    )

    bg_all = group_rows(branch_grad)
    (gated_grad,) = product(
        [(bg_all, w_rest, "nn", 2 * tiles)], [(everyone, part, F32)], lambda acc: (acc,)
    )
    gate_grad, wkv_grad, ends = call(
        gate_kernel,
        ins="tttttp",
        outs=[("t", BF16), ("t", F32), ("x", F32)],
        args=(gated_grad, gate_pre, wkv, receipt, log_decay, wkv_rows),
    )
    val_kept, val_got = far_split(val_pair)
    keys_at, open_bits = list(range(size)), size - 1
    stage_arrays = [ends.reshape(size * high, part)]
    for index, (mask, merges) in enumerate(stages):
        last = index + 1 == len(stages)
        after_keys = keys_at
        for bit in merges:
            after_keys = [g for g in after_keys if not g & bit]

        def backward_stage(
            who, late, *arrays, mask=mask, merges=merges, groups=keys_at, bits=open_bits, last=last
        ):
            marks = [arrays[-1][i * 8 : i * 8 + 1] for i in range(arrays[-1].shape[0] // 8)]
            if mask is None:
                cut = [arrays[0][k * high : k * high + SPAN] for k in range(size)]
                total = dict(enumerate(swap_members(who, cut)))
                chunks = [neutral() for _ in range(size)]
            else:
                total = {g: arrays[0][i * SPAN : (i + 1) * SPAN] for i, g in enumerate(groups)}
                chunks = unpack(arrays[1], size)
                other = {
                    g: arrays[2][i * SPAN : (i + 1) * SPAN].astype(F32)
                    for i, g in enumerate(groups)
                }
                here = dict(zip(groups, marks))
                there = dict(zip(groups, marks[len(groups) :]))
                marks = marks[2 * len(groups) :]
                early = late == 0
                chunks = [
                    pick(
                        early,
                        (d * there[m & bits], d * other[m & bits] + v),
                        (d, v),
                    )
                    for m, (d, v) in enumerate(chunks)
                ]
                total = {
                    g: jnp.where(
                        early,
                        total[g] + here[g] * other[g],
                        other[g] + there[g] * total[g],
                    )
                    for g in groups
                }
            for bit in merges:
                here = dict(zip(total, marks))
                marks = marks[len(total) :]
                chunks = [
                    (d, v)
                    if m & bit
                    else (d * here[(m & bits) | bit], d * total[(m & bits) | bit] + v)
                    for m, (d, v) in enumerate(chunks)
                ]
                total = {
                    g: total[g] + here[g] * total[g | bit] for g in total if not g & bit
                }
                bits ^= bit
            joint = jnp.concatenate(list(total.values()), axis=0)
            if last:
                grads = swap_members(who, [v for _, v in chunks])
                return jnp.concatenate(grads, axis=0), joint.T
            return joint, pack(chunks), joint

        if last:
            outs = [(size * SPAN, part, F32), (part, SPAN, F32)]
            grad_out, first_grad = local(
                backward_stage, outs, *stage_arrays, decays[index], scalar=flags_of(mask)
            )
            grad_out = grad_out.reshape(size, SPAN, part)
        else:
            outs = [
                (len(after_keys) * SPAN, part, F32),
                (size * high, part, F32),
                (len(after_keys) * SPAN, part, BF16),
            ]
            total, chunks, sent = local(
                backward_stage, outs, *stage_arrays, decays[index], scalar=flags_of(mask)
            )
            if mask == (2 if fast else 4):
                sent, val_got = tie(sent, val_got)
            stage_arrays = [total, chunks, trade(sent, stages[index + 1][0])]
        keys_at = after_keys
        for bit in merges:
            open_bits ^= bit
    out_grads = team_products((bg_all, gated), (recv_all, rg_all), (mixed_all[3], gate_grad))
    grad_out, out_grads = tie(grad_out, out_grads)
    out_pair = square_sum(out_grads)

    d_receipt, d_keys, d_values, d_decay, extra = call(
        backward_kernel,
        ins="tttttssp",
        outs=[("t", BF16)] * 4 + [("e", F32)],
        args=(receipt, keys, values, log_decay, wkv_grad, state_in, grad_out, wkv_rows),
    )
    grads = [d_keys, d_values, d_receipt, gate_grad]
    kept, sent = crossing_sum(
        *[(grads[c], w_rest if c > 1 else w_kv, c % 2) for c in range(4)]
    )
    main_grads = team_products(
        (mixed_all[0], d_keys), (mixed_all[1], d_values), (mixed_all[2], d_receipt)
    )

    def latent_back(grad, up):
        kept, sent = halves(nn(grad, up))
        return jnp.concatenate(kept, axis=0), jnp.concatenate(sent, axis=0)

    latent_mine, latent_more = group_sum(
        *local(
            latent_back, [(2 * step, DRANK, F32), (2 * step, DRANK, BF16)], d_decay, w_dup
        )
    )
    key_kept, key_got = far_split(key_pair)
    sent, main_grads, latent_more, key_got = tie(sent, main_grads, latent_more, key_got)
    main_pair = square_sum(main_grads)
    mixed_mine, mixed_more = group_sum(kept, sent)
    mixed_more, out_pair = tie(mixed_more, out_pair)
    out_kept, out_got = far_split(out_pair)
    val_sum, key_sum = far_add(val_kept, val_got), far_add(key_kept, key_got)
    rest_grad, delta_grad, top_one, cols_mix, down_grad, up_grad, ddown_grad = mixes_back(
        mixed_mine,
        mixed_more,
        latent_mine,
        latent_more,
        delta,
        mix_tanh,
        decay_tanh,
        blend,
        mixed_zero,
        w_down,
        w_up,
        w_ddown,
        vec,
    )
    rest_grad, main_pair, out_got = tie(rest_grad, main_pair, out_got)
    out_sum = far_add(out_kept, out_got)

    def norm_one_back(last, rest, shifted, arrived, normal, scale, middle, vec):
        below = jnp.where(last == 1, jnp.zeros_like(arrived[:1]), arrived[:1])
        grad = rest + rows_below(shifted, below)
        out = middle + norm_back(grad, vec[0:1], normal, scale[:, :1])
        cols = padded([column_sum(grad * normal), column_sum(grad)])
        return take_lanes(out, from_spans), cols

    block_input_gradient, cols_one = local(
        norm_one_back,
        [whole, (8, width, F32)],
        rest_grad,
        delta_grad,
        neighbour(top_one, -1),
        normal_one,
        scale_one,
        middle_grad,
        vec,
        scalar=last_flag,
    )
    main_kept, main_got = far_split(main_pair)


    def spread(value):
        zero = jnp.zeros((width, value.shape[1]), F32)
        return lax.dynamic_update_slice_in_dim(zero, value, member * part, axis=0)

    vec_low = jnp.concatenate([cols_one[:2], cols_mix[:6], cols_two[:4]], axis=0)
    vec_head = jnp.concatenate(
        [jnp.sum(extra[:, :2], axis=0), jnp.sum(ends[:, SPAN : SPAN + 2], axis=0)], axis=0
    )
    by_feature = jnp.concatenate([down_grad, up_grad, ddown_grad, vec_low.T], axis=1)
    by_channel = spread(jnp.concatenate([tn(d_decay, dh_all), vec_head.T], axis=1))
    low, main_got = cube_sum(
        jnp.concatenate(
            [to_cube(by_feature), by_channel.reshape(*[2] * len(all_masks), rows, -1)], axis=-1
        ),
        BF16,
        main_got,
    )
    main_sum = far_add(main_kept, main_got)

    def column_parts(value):
        return [value[:, c * part : (c + 1) * part] for c in range(3)]

    out_cols, main_cols = column_parts(out_sum), column_parts(main_sum)
    holder = lax.div(me * rows, part)

    def rows_of(who):
        mine = lax.dynamic_slice_in_dim(first_grad, lax.rem(who * rows, part), rows, axis=0)
        high = lax.reduce_precision(mine, 8, 7)
        return jnp.concatenate([high, mine - high], axis=1).astype(BF16)

    feedforward_gradient, handed = hand_rows(
        [[key_sum], [out_cols[1]], [val_sum]],
        [rows_of(jnp.bitwise_xor(me, flips(k))) for k in range(size)],
    )
    state_rows = handed[0]
    for k in range(1, size):
        state_rows = jnp.where(holder == (member ^ k), handed[k], state_rows)
    initial_state_gradient = state_rows[:, :SPAN] + state_rows[:, SPAN:]
    mixing_gradient = hand_rows([[m] for m in main_cols] + [[out_cols[2]], [out_cols[0]]])

    vec_at = decay_up + 12
    lowrank_gradient = jnp.concatenate(
        [low[:, :decay_up], low[:, vec_at : vec_at + DRANK]], axis=1
    )
    vectors_gradient = jnp.concatenate(
        [low[:, decay_up : decay_up + 8], low[:, vec_at + DRANK :], low[:, decay_up + 8 : vec_at]],
        axis=1,
    )
    return (
        block_output.reshape(1, step, width),
        block_input_gradient.reshape(1, step, width),
        initial_state_gradient,
        mixing_gradient,
        lowrank_gradient,
        vectors_gradient,
        feedforward_gradient,
    )


def solution(mesh):
    rowwise = P("seq", None)
    tokenwise = P(None, "seq", None)
    return jax.shard_map(
        functools.partial(on_device, mesh.shape["seq"]),
        mesh=mesh,
        in_specs=(tokenwise, P(), rowwise, rowwise, rowwise, rowwise, rowwise, tokenwise),
        out_specs=(tokenwise, tokenwise, rowwise, rowwise, rowwise, rowwise, rowwise),
        check_vma=False,
    )
```

profile of v0, /device:TPU:0, one launch (start us, length us, event | category | flops | bytes accessed | tf_op | source)
XLA Modules:
  0.0 925.2 jit_solution(13157470327241201155)
XLA Ops:
  25.1 13.4 %collective-permute-done.4 = f32[2,64,144]{2,1,0:T(8,128)S(1)} collective-permute-done((f32[2,64,144]{2,1,0:T(8,128)S(1)}, f32[2,64,144]{2,1,0:T(8,128)S(1)}, u32[]{:S(2)}, u32[]{:S(2)}) %collective-permute-start.4) | collective-permute-done | bytes 73760 | tf_op jit(solution)/shard_map/ppermute | solution.py:667
  52.9 9.9 %collective-permute-done.8 = f32[2,2,2,64,144]{4,3,2,1,0:T(8,128)S(1)} collective-permute-done((f32[2,2,2,64,144]{4,3,2,1,0:T(8,128)S(1)}, f32[2,2,2,64,144]{4,3,2,1,0:T(8,128)S(1)}, u32[]{:S(2)}, u32[]{:S(2)}) %collective-permute-start.8) | collective-permute-done | bytes 294944 | tf_op jit(solution)/shard_map/ppermute | solution.py:667
  76.8 24.0 %collective-permute-done.15 = bf16[256,1024]{1,0:T(8,128)(2,1)S(1)} collective-permute-done((bf16[256,1024]{1,0:T(8,128)(2,1)S(1)}, bf16[256,1024]{1,0:T(8,128)(2,1)S(1)}, u32[]{:S(2)}, u32[]{:S(2)}) %collective-permute-start.15) | collective-permute-done | bytes 524320 | tf_op jit(solution)/shard_map/ppermute | solution.py:667
  110.1 16.4 %shard_map.137 = (bf16[512,2048]{1,0:T(8,128)(2,1)}, bf16[512,2048]{1,0:T(8,128)(2,1)}, bf16[512,2048]{1,0:T(8,128)(2,1)}, bf16[512,2048]{1,0:T(8,128)(2,1)}, bf...) custom-call(s32[4]{0:T(128)} %add_convert_fusion.4.open_ref, ...), custom_call_target="tpu_custom_call" | custom-call | tf_op jit(solution)/shard_map/pallas_call | solution.py:386
  126.5 12.2 %collective-permute-done.16 = bf16[256,1536]{1,0:T(8,128)(2,1)} collective-permute-done((bf16[256,1536]{1,0:T(8,128)(2,1)S(1)}, bf16[256,1536]{1,0:T(8,128)(2,1)}, u32[]{:S(2)}, u32[]{:S(2)}) %collective-permute-start.16) | collective-permute-done | bytes 786464 | tf_op jit(solution)/shard_map/ppermute | solution.py:667
  142.4 23.9 %collective-permute-done.17 = bf16[128,4096]{1,0:T(8,128)(2,1)S(1)} collective-permute-done((bf16[128,4096]{1,0:T(8,128)(2,1)S(1)}, bf16[128,4096]{1,0:T(8,128)(2,1)S(1)}, u32[]{:S(2)}, u32[]{:S(2)}) %collective-permute-start.17) | collective-permute-done | bytes 1048608 | tf_op jit(solution)/shard_map/ppermute | solution.py:667
  200.2 8.3 collective-permute-done.19.refs_3_
  211.4 22.1 %collective-permute-done.20 = bf16[256,2304]{1,0:T(8,128)(2,1)} collective-permute-done((bf16[256,2304]{1,0:T(8,128)(2,1)}, bf16[256,2304]{1,0:T(8,128)(2,1)}, u32[]{:S(2)}, u32[]{:S(2)}) %collective-permute-start.20) | collective-permute-done | bytes 1179680 | tf_op jit(solution)/shard_map/ppermute | solution.py:667
  263.6 14.3 %shard_map.146 = (f32[512,512]{1,0:T(8,128)S(1)}, bf16[512,512]{1,0:T(8,128)(2,1)S(1)}) custom-call(f32[512,512]{1,0:T(8,128)S(1)} %copy-done.9, f32[512,512]{1,0:T(8,128)S(1)} %copy-done.7, f32[512,512]{1,0:T(8,128)S(1)} %copy-done.8, f32[512,512]{1,0:T(8,128)} %shard_map.140.w_ref, f32[512,512]{1,0:T(8,128)} %get-tuple-element.173.g_ref, ...), custom_call_target="tpu_custom_call" | custom-call | tf_op jit(solution)/shard_map/pallas_call | solution.py:222
  279.7 16.6 %collective-permute-done.23 = bf16[256,1792]{1,0:T(8,128)(2,1)} collective-permute-done((bf16[256,1792]{1,0:T(8,128)(2,1)S(1)}, bf16[256,1792]{1,0:T(8,128)(2,1)}, u32[]{:S(2)}, u32[]{:S(2)}) %collective-permute-start.23) | collective-permute-done | bytes 917536 | tf_op jit(solution)/shard_map/ppermute | solution.py:667
  311.0 14.2 %collective-permute-done.25.refs_2_ = bf16[128,2048]{1,0:T(8,128)(2,1)S(1)} collective-permute-done((bf16[128,2048]{1,0:T(8,128)(2,1)}, bf16[128,2048]{1,0:T(8,128)(2,1)S(1)}, u32[]{:S(2)}, u32[]{:S(2)}) %collective-permute-start.25) | collective-permute-done | bytes 524320 | tf_op jit(solution)/shard_map/ppermute | solution.py:667
  341.9 12.7 %collective-permute-done.27.refs_1_ = bf16[128,2048]{1,0:T(8,128)(2,1)S(1)} collective-permute-done((bf16[128,2048]{1,0:T(8,128)(2,1)S(1)}, bf16[128,2048]{1,0:T(8,128)(2,1)S(1)}, u32[]{:S(2)}, u32[]{:S(2)}) %collective-permute-start.27) | collective-permute-done | bytes 524320 | tf_op jit(solution)/shard_map/ppermute | solution.py:667
  354.7 10.1 %collective-permute-done.29.refs_1_ = bf16[128,2048]{1,0:T(8,128)(2,1)S(1)} collective-permute-done((bf16[128,2048]{1,0:T(8,128)(2,1)S(1)}, bf16[128,2048]{1,0:T(8,128)(2,1)S(1)}, u32[]{:S(2)}, u32[]{:S(2)}) %collective-permute-start.29) | collective-permute-done | bytes 524320 | tf_op jit(solution)/shard_map/ppermute | solution.py:667
  380.5 9.0 shard_map.152
  389.5 24.2 %all-gather.11.cloned.1.call-done.refs_1_ = bf16[2048,1792]{1,0:T(8,128)(2,1)} async-done(((bf16[512,1792]{1,0:T(8,128)(2,1)}), bf16[2048,1792]{1,0:T(8,128)(2,1)}) %all-gather.11.cloned.1.call-update) | async-done | bytes 7340048 | tf_op jit(solution)/shard_map/all_gather | solution.py:773
  437.4 12.2 %collective-permute-done.32.more_ref = bf16[128,2048]{1,0:T(8,128)(2,1)S(1)} collective-permute-done((bf16[128,2048]{1,0:T(8,128)(2,1)}, bf16[128,2048]{1,0:T(8,128)(2,1)S(1)}, u32[]{:S(2)}, u32[]{:S(2)}) %collective-permute-start.32) | collective-permute-done | bytes 524320 | tf_op jit(solution)/shard_map/ppermute | solution.py:667
  457.4 12.0 %collective-permute-done.35.refs_1_ = bf16[128,2048]{1,0:T(8,128)(2,1)S(1)} collective-permute-done((bf16[128,2048]{1,0:T(8,128)(2,1)}, bf16[128,2048]{1,0:T(8,128)(2,1)S(1)}, u32[]{:S(2)}, u32[]{:S(2)}) %collective-permute-start.35) | collective-permute-done | bytes 524320 | tf_op jit(solution)/shard_map/ppermute | solution.py:667
  489.9 9.0 shard_map.160.refs_1_.refs_0_
  508.5 8.4 shard_map.162
  532.7 8.8 collective-permute-done.40.refs_1_
  541.6 10.9 %collective-permute-done.42.refs_3_ = bf16[128,2048]{1,0:T(8,128)(2,1)S(1)} collective-permute-done((bf16[128,2048]{1,0:T(8,128)(2,1)}, bf16[128,2048]{1,0:T(8,128)(2,1)S(1)}, u32[]{:S(2)}, u32[]{:S(2)}) %collective-permute-start.42) | collective-permute-done | bytes 524320 | tf_op jit(solution)/shard_map/ppermute | solution.py:667
  569.0 11.3 %collective-permute-done.44.refs_1_ = bf16[128,2048]{1,0:T(8,128)(2,1)S(1)} collective-permute-done((bf16[128,2048]{1,0:T(8,128)(2,1)}, bf16[128,2048]{1,0:T(8,128)(2,1)S(1)}, u32[]{:S(2)}, u32[]{:S(2)}) %collective-permute-start.44) | collective-permute-done | bytes 524320 | tf_op jit(solution)/shard_map/ppermute | solution.py:667
  597.8 12.2 %shard_map.170 = (bf16[512,512]{1,0:T(8,128)(2,1)S(1)}, f32[512,512]{1,0:T(8,128)S(1)}, f32[4,72,512]{2,1,0:T(8,128)S(1)}) custom-call(f32[512,512]{1,0:T(8,128)S(1)} %copy-done.15, f32[512,512]{1,0:T(8,128)S(1)} %copy-done.16, f32[512,512]{1,0:T(8,128)S(1)} %copy-done.29, f32[512,512]{1,0:T(8,128)} %get-tuple-element.164.r_ref, ...), custom_call_target="tpu_custom_call" | custom-call | tf_op jit(solution)/shard_map/pallas_call | solution.py:222
  641.9 9.4 %shard_map.175 = bf16[8,256,1536]{2,1,0:T(8,128)(2,1)} custom-call(s32[8]{0:T(128)S(1)} %iota.14._, bf16[512,2048]{1,0:T(8,128)(2,1)S(1)} %copy-done.4, bf16[512,512]{1,0:T(8,128)(2,1)S(1)} %copy-done.27, bf16[512,2048]{1,0:T(8,128)(2,1)S(1)} %copy-done.2, bf16[512,512]{1,0:T(8,128)(2,1)S(1)} %copy-done.14, ...), custom_call_target="tpu_custom_call" | custom-call | tf_op jit(solution)/shard_map/pallas_call | solution.py:248
  661.3 14.8 %shard_map.176 = (bf16[512,512]{1,0:T(8,128)(2,1)S(1)}, bf16[512,512]{1,0:T(8,128)(2,1)S(1)}, bf16[512,512]{1,0:T(8,128)(2,1)S(1)}, bf16[512,512]{1,0:T(8,128)(2,1)S(1)}, f32[4,8,512]{2,1,0:T(8,128)S(1)}) custom-call(f32[512,512]{1,0:T(8,128)S(1)} %copy-done.10, f32[512,512]{1,0:T(8,128)S(1)} %copy-done.7, f32[512,512]{1,0:T(8,128)} %get-tuple-element.171.v_ref, ...), custom_call_target="tpu_custom_call" | custom-call | tf_op jit(solution)/shard_map/pallas_call | solution.py:222
  686.5 9.4 %shard_map.178 = bf16[8,256,1536]{2,1,0:T(8,128)(2,1)} custom-call(s32[8]{0:T(128)S(1)} %iota.15._, bf16[512,2048]{1,0:T(8,128)(2,1)S(1)} %copy-done.11, bf16[512,512]{1,0:T(8,128)(2,1)S(1)} %get-tuple-element.249.refs_0_.refs_1_, bf16[512,2048]{1,0:T(8,128)(2,1)S(1)} %copy-done.12, bf16[512,512]{1,0:T(8,128)(2,1)S(1)} %get-tuple-element.250.refs_2_.refs_3_, ...), custom_call_target="tpu_custom_call" | custom-call | tf_op jit(solution)/shard_map/pallas_call | solution.py:248
  695.9 11.1 %shard_map.177 = (f32[1024,2048]{1,0:T(8,128)}, bf16[1024,2048]{1,0:T(8,128)(2,1)}) custom-call(bf16[512,512]{1,0:T(8,128)(2,1)} %copy-done.20, bf16[2048,1024]{1,0:T(8,128)(2,1)} %all-gather.7.cloned.1.call-done.refs_1_.refs_3_, bf16[512,512]{1,0:T(8,128)(2,1)} %copy-done.21, bf16[2048,1024]{1,0:T(8,128)(2,1)} %all-gather.7.cloned.1.call-done.refs_1_.refs_3_, ...), custom_call_target="tpu_custom_call" | custom-call | tf_op jit(solution)/shard_map/pallas_call | solution.py:428
  727.8 45.0 %collective-permute-done.54.got_ref = bf16[512,2048]{1,0:T(8,128)(2,1)} collective-permute-done((bf16[512,2048]{1,0:T(8,128)(2,1)}, bf16[512,2048]{1,0:T(8,128)(2,1)}, u32[]{:S(2)}, u32[]{:S(2)}) %collective-permute-start.54) | collective-permute-done | bytes 2097184 | tf_op jit(solution)/shard_map/ppermute | solution.py:667
  780.4 12.7 %shard_map.182 = (f32[128,2048]{1,0:T(8,128)}, f32[128,2048]{1,0:T(8,128)}, f32[8,2048]{1,0:T(8,128)}, f32[8,2048]{1,0:T(8,128)}, f32[2048,160]{1,0:T(8,128)}, /*index=5*/f32[2048,160]{1,0:T(8,128)}, f32[2048,64]{1,0:T(8,128)}) custom-call(f32[512,2048]{1,0:T(8,128)} %get-tuple-element.260.kept_ref, bf16[512,2048]{1,0:T(8,128)(2,1)} %collective-permute-done.54.got_ref, ...), custom_call_target="tpu_custom_call" | custom-call | tf_op jit(solution)/shard_map/pallas_call | solution.py:597
  794.8 8.7 reduce-scatter.11.cloned.1.call-done
  837.4 35.6 %collective-permute-done.57 = bf16[128,4224]{1,0:T(8,128)(2,1)} collective-permute-done((bf16[128,4224]{1,0:T(8,128)(2,1)}, bf16[128,4224]{1,0:T(8,128)(2,1)}, u32[]{:S(2)}, u32[]{:S(2)}) %collective-permute-start.57) | collective-permute-done | bytes 1081376 | tf_op jit(solution)/shard_map/ppermute | solution.py:667
  898.3 10.2 %collective-permute-done.62 = bf16[128,2560]{1,0:T(8,128)(2,1)} collective-permute-done((bf16[128,2560]{1,0:T(8,128)(2,1)}, bf16[128,2560]{1,0:T(8,128)(2,1)}, u32[]{:S(2)}, u32[]{:S(2)}) %collective-permute-start.62) | collective-permute-done | bytes 655392 | tf_op jit(solution)/shard_map/ppermute | solution.py:667
  (549 shorter events, 436.0 us)
Async XLA Ops:
  7.2 164.4 %all-gather.7.cloned.1.call-start = ((), (), s32[]{:S(2)}) async-start(), calls=%async_computation.5 | async-start | bytes 5242880 | tf_op jit(solution)/shard_map/all_gather | solution.py:773
  18.7 44.4 %collective-permute-start.13 = (bf16[144,2048]{1,0:T(8,128)(2,1)S(1)}, bf16[144,2048]{1,0:T(8,128)(2,1)S(1)}, u32[]{:S(2)}, u32[]{:S(2)}) collective-permute-start(bf16[144,2048]{1,0:T(8,128)(2,1)S(1)} %shard_map.135.refs_0_), channel_id=1, source_target_pairs={{0,8},{1,9},{2,10},{3,11},{4,12},{5,13},{6,14},{7,15},{8,0},{9,1},... | collective-permute-start | bytes 1769480 | tf_op jit(solution)/shard_map/ppermute | solution.py:667
  24.7 15.9 %collective-permute-start.2 = (bf16[2,64,384]{2,1,0:T(8,128)(2,1)S(1)}, bf16[2,64,384]{2,1,0:T(8,128)(2,1)S(1)}, u32[]{:S(2)}, u32[]{:S(2)}) collective-permute-start(bf16[2,64,384]{2,1,0:T(8,128)(2,1)S(1)} %pad_maximum_fusion.37), channel_id=1, source_target_pairs={{0,8},{1,9},{2,10},{3,11},{4,12},{5,13},{6,14},{7,15},{8,0},{9,1},... | collective-permute-start | bytes 294920 | tf_op jit(solution)/shard_map/ppermute | solution.py:667
  40.9 22.8 %collective-permute-start.5 = (bf16[128,2560]{1,0:T(8,128)(2,1)S(1)}, bf16[128,2560]{1,0:T(8,128)(2,1)S(1)}, u32[]{:S(2)}, u32[]{:S(2)}) collective-permute-start(bf16[128,2560]{1,0:T(8,128)(2,1)S(1)} %pad_maximum_fusion.20), channel_id=1, source_target_pairs={{0,8},{1,9},{2,10},{3,11},{4,12},{5,13},{6,14},{7,15},{8,0},{9,1},... | collective-permute-start | bytes 1966088 | tf_op jit(solution)/shard_map/ppermute | solution.py:667
  51.3 17.5 %collective-permute-start.11 = (bf16[2,2,2,64,384]{4,3,2,1,0:T(8,128)(2,1)S(1)}, bf16[2,2,2,64,384]{4,3,2,1,0:T(8,128)(2,1)S(1)}, u32[]{:S(2)}, u32[]{:S(2)}) collective-permute-start(bf16[2,2,2,64,384]{4,3,2,1,0:T(8,128)(2,1)S(1)} %pad_maximum_fusion.29), channel_id=1, source_target_pairs={{0,2},{1,3},{2,0},{3,1},{4,6},{5,7},{6,4},{7,5},{8,10},{9,11},{10,... | collective-permute-start | bytes 1179656 | tf_op jit(solution)/shard_map/ppermute | solution.py:667
  74.6 26.2 %collective-permute-start.15 = (bf16[256,1024]{1,0:T(8,128)(2,1)S(1)}, bf16[256,1024]{1,0:T(8,128)(2,1)S(1)}, u32[]{:S(2)}, u32[]{:S(2)}) collective-permute-start(bf16[256,1024]{1,0:T(8,128)(2,1)S(1)} %slice.316), channel_id=1, source_target_pairs={{0,16},{1,17},{2,18},{3,19},{4,20},{5,21},{6,22},{7,23},{8,24},{9,... | collective-permute-start | bytes 1572872 | tf_op jit(solution)/shard_map/ppermute | solution.py:667
  101.9 153.9 %all-gather.5.cloned.1.call-start = ((), (), s32[]{:S(2)}) async-start(), calls=%async_computation.4 | async-start | bytes 7864320 | tf_op jit(solution)/shard_map/all_gather | solution.py:773
  102.0 36.7 %collective-permute-start.16 = (bf16[256,1536]{1,0:T(8,128)(2,1)S(1)}, bf16[256,1536]{1,0:T(8,128)(2,1)}, u32[]{:S(2)}, u32[]{:S(2)}) collective-permute-start(bf16[256,1536]{1,0:T(8,128)(2,1)S(1)} %slice.317), channel_id=1, source_target_pairs={{0,16},{1,17},{2,18},{3,19},{4,20},{5,21},{6,22},{7,23},{8,24},{9,... | collective-permute-start | bytes 2359304 | tf_op jit(solution)/shard_map/ppermute | solution.py:667
  141.2 231.9 %all-gather.9.cloned.1.call-start = ((), (), s32[]{:S(2)}) async-start(), calls=%async_computation.6 | async-start | bytes 11796480 | tf_op jit(solution)/shard_map/all_gather | solution.py:773
  142.4 24.0 %collective-permute-start.17 = (bf16[128,4096]{1,0:T(8,128)(2,1)S(1)}, bf16[128,4096]{1,0:T(8,128)(2,1)S(1)}, u32[]{:S(2)}, u32[]{:S(2)}) collective-permute-start(bf16[128,4096]{1,0:T(8,128)(2,1)S(1)} %maximum_maximum_fusion), channel_id=1, source_target_pairs={{0,8},{1,9},{2,10},{3,11},{4,12},{5,13},{6,14},{7,15},{8,0},{9,1},... | collective-permute-start | bytes 3145736 | tf_op jit(solution)/shard_map/ppermute | solution.py:667
  179.3 54.2 %collective-permute-start.20 = (bf16[256,2304]{1,0:T(8,128)(2,1)}, bf16[256,2304]{1,0:T(8,128)(2,1)}, u32[]{:S(2)}, u32[]{:S(2)}) collective-permute-start(bf16[256,2304]{1,0:T(8,128)(2,1)} %slice.325), channel_id=1, source_target_pairs={{0,16},{1,17},{2,18},{3,19},{4,20},{5,21},{6,22},{7,23},{8,24},{9,... | collective-permute-start | bytes 3538952 | tf_op jit(solution)/shard_map/ppermute | solution.py:667
  236.5 177.2 %all-gather.11.cloned.1.call-start = ((), (), s32[]{:S(2)}) async-start(), calls=%async_computation.7 | async-start | bytes 9175040 | tf_op jit(solution)/shard_map/all_gather | solution.py:773
  255.3 41.0 %collective-permute-start.23 = (bf16[256,1792]{1,0:T(8,128)(2,1)S(1)}, bf16[256,1792]{1,0:T(8,128)(2,1)}, u32[]{:S(2)}, u32[]{:S(2)}) collective-permute-start(bf16[256,1792]{1,0:T(8,128)(2,1)S(1)} %slice.327), channel_id=1, source_target_pairs={{0,16},{1,17},{2,18},{3,19},{4,20},{5,21},{6,22},{7,23},{8,24},{9,... | collective-permute-start | bytes 2752520 | tf_op jit(solution)/shard_map/ppermute | solution.py:667
  299.0 284.6 %reduce-scatter.5.cloned.1.call-start = ((), (), s32[]{:S(2)}) async-start(), calls=%async_computation.8 | async-start | bytes 9175040 | tf_op jit(solution)/shard_map/reduce_scatter | solution.py:783
  336.3 18.3 %collective-permute-start.27 = (bf16[128,2048]{1,0:T(8,128)(2,1)S(1)}, bf16[128,2048]{1,0:T(8,128)(2,1)S(1)}, u32[]{:S(2)}, u32[]{:S(2)}) collective-permute-start(bf16[128,2048]{1,0:T(8,128)(2,1)S(1)} %get-tuple-element.386.refs_0_), channel_id=1, source_target_pairs={{0,8},{1,9},{2,10},{3,11},{4,12},{5,13},{6,14},{7,15},{8,0},{9,1},... | collective-permute-start | bytes 1572872 | tf_op jit(solution)/shard_map/ppermute | solution.py:667
  341.8 23.1 %collective-permute-start.29 = (bf16[128,2048]{1,0:T(8,128)(2,1)S(1)}, bf16[128,2048]{1,0:T(8,128)(2,1)S(1)}, u32[]{:S(2)}, u32[]{:S(2)}) collective-permute-start(bf16[128,2048]{1,0:T(8,128)(2,1)S(1)} %get-tuple-element.385.refs_0_), channel_id=1, source_target_pairs={{0,8},{1,9},{2,10},{3,11},{4,12},{5,13},{6,14},{7,15},{8,0},{9,1},... | collective-permute-start | bytes 1572872 | tf_op jit(solution)/shard_map/ppermute | solution.py:667
  456.8 16.9 %collective-permute-start.37 = (bf16[256,512]{1,0:T(8,128)(2,1)S(1)}, bf16[256,512]{1,0:T(8,128)(2,1)S(1)}, u32[]{:S(2)}, u32[]{:S(2)}) collective-permute-start(bf16[256,512]{1,0:T(8,128)(2,1)S(1)} %concatenate.200), channel_id=1, source_target_pairs={{0,8},{1,9},{2,10},{3,11},{4,12},{5,13},{6,14},{7,15},{8,0},{9,1},... | collective-permute-start | bytes 786440 | tf_op jit(solution)/shard_map/ppermute | solution.py:667
  489.8 166.8 %reduce-scatter.7.cloned.1.call-start = ((), (), s32[]{:S(2)}) async-start(), calls=%async_computation.9 | async-start | bytes 9175040 | tf_op jit(solution)/shard_map/reduce_scatter | solution.py:783
  508.4 264.4 %reduce-scatter.9.cloned.1.call-start = ((), (), s32[]{:S(2)}) async-start(), calls=%async_computation.10 | async-start | bytes 7864320 | tf_op jit(solution)/shard_map/reduce_scatter | solution.py:783
  532.4 20.1 %collective-permute-start.42 = (bf16[128,2048]{1,0:T(8,128)(2,1)}, bf16[128,2048]{1,0:T(8,128)(2,1)S(1)}, u32[]{:S(2)}, u32[]{:S(2)}) collective-permute-start(bf16[128,2048]{1,0:T(8,128)(2,1)} %get-tuple-element.221), channel_id=1, source_target_pairs={{0,8},{1,9},{2,10},{3,11},{4,12},{5,13},{6,14},{7,15},{8,0},{9,1},... | collective-permute-start | bytes 1572872 | tf_op jit(solution)/shard_map/ppermute | solution.py:667
  585.8 43.5 %collective-permute-start.47 = (bf16[256,1792]{1,0:T(8,128)(2,1)}, bf16[256,1792]{1,0:T(8,128)(2,1)}, u32[]{:S(2)}, u32[]{:S(2)}) collective-permute-start(bf16[256,1792]{1,0:T(8,128)(2,1)} %constant_dynamic-slice_fusion.10), channel_id=1, source_target_pairs={{0,16},{1,17},{2,18},{3,19},{4,20},{5,21},{6,22},{7,23},{8,24},{9,... | collective-permute-start | bytes 2752520 | tf_op jit(solution)/shard_map/ppermute | solution.py:667
  654.0 149.5 %reduce-scatter.11.cloned.1.call-start = ((), (), s32[]{:S(2)}) async-start(), calls=%async_computation.11 | async-start | bytes 7864320 | tf_op jit(solution)/shard_map/reduce_scatter | solution.py:783
  658.8 48.3 %collective-permute-start.52 = (bf16[256,1792]{1,0:T(8,128)(2,1)}, bf16[256,1792]{1,0:T(8,128)(2,1)}, u32[]{:S(2)}, u32[]{:S(2)}) collective-permute-start(bf16[256,1792]{1,0:T(8,128)(2,1)} %constant_dynamic-slice_fusion.9), channel_id=1, source_target_pairs={{0,16},{1,17},{2,18},{3,19},{4,20},{5,21},{6,22},{7,23},{8,24},{9,... | collective-permute-start | bytes 2752520 | tf_op jit(solution)/shard_map/ppermute | solution.py:667
  683.1 23.9 %collective-permute-start.51 = (bf16[128,64]{1,0:T(8,128)(2,1)}, bf16[128,64]{1,0:T(8,128)(2,1)S(1)}, u32[]{:S(2)}, u32[]{:S(2)}) collective-permute-start(bf16[128,64]{1,0:T(8,128)(2,1)} %get-tuple-element.257), channel_id=1, source_target_pairs={{0,8},{1,9},{2,10},{3,11},{4,12},{5,13},{6,14},{7,15},{8,0},{9,1},... | collective-permute-start | bytes 49160 | tf_op jit(solution)/shard_map/ppermute | solution.py:667
  724.7 48.1 %collective-permute-start.54 = (bf16[512,2048]{1,0:T(8,128)(2,1)}, bf16[512,2048]{1,0:T(8,128)(2,1)}, u32[]{:S(2)}, u32[]{:S(2)}) collective-permute-start(bf16[512,2048]{1,0:T(8,128)(2,1)} %get-tuple-element.261), channel_id=1, source_target_pairs={{0,8},{1,9},{2,10},{3,11},{4,12},{5,13},{6,14},{7,15},{8,0},{9,1},... | collective-permute-start | bytes 6291464 | tf_op jit(solution)/shard_map/ppermute | solution.py:667
  774.9 36.9 %collective-permute-start.55 = (bf16[256,1536]{1,0:T(8,128)(2,1)}, bf16[256,1536]{1,0:T(8,128)(2,1)}, u32[]{:S(2)}, u32[]{:S(2)}) collective-permute-start(bf16[256,1536]{1,0:T(8,128)(2,1)} %constant_dynamic-slice_fusion.8), channel_id=1, source_target_pairs={{0,16},{1,17},{2,18},{3,19},{4,20},{5,21},{6,22},{7,23},{8,24},{9,... | collective-permute-start | bytes 2359304 | tf_op jit(solution)/shard_map/ppermute | solution.py:667
  793.1 21.0 %collective-permute-start.56 = (f32[8,2048]{1,0:T(8,128)}, f32[8,2048]{1,0:T(8,128)S(1)}, u32[]{:S(2)}, u32[]{:S(2)}) collective-permute-start(f32[8,2048]{1,0:T(8,128)} %get-tuple-element.276), channel_id=1, source_target_pairs={{1,0},{2,1},{3,2},{4,3},{5,4},{6,5},{7,6},{8,7},{9,8},{10,9},{11,1... | collective-permute-start | bytes 196616 | tf_op jit(solution)/shard_map/ppermute | solution.py:736
  830.1 42.9 %collective-permute-start.57 = (bf16[128,4224]{1,0:T(8,128)(2,1)}, bf16[128,4224]{1,0:T(8,128)(2,1)}, u32[]{:S(2)}, u32[]{:S(2)}) collective-permute-start(bf16[128,4224]{1,0:T(8,128)(2,1)} %pad_maximum_fusion.10), channel_id=1, source_target_pairs={{0,8},{1,9},{2,10},{3,11},{4,12},{5,13},{6,14},{7,15},{8,0},{9,1},... | collective-permute-start | bytes 3244040 | tf_op jit(solution)/shard_map/ppermute | solution.py:667
  832.2 43.2 %collective-permute-start.61 = (bf16[256,1536]{1,0:T(8,128)(2,1)}, bf16[256,1536]{1,0:T(8,128)(2,1)}, u32[]{:S(2)}, u32[]{:S(2)}) collective-permute-start(bf16[256,1536]{1,0:T(8,128)(2,1)} %constant_dynamic-slice_fusion.4), channel_id=1, source_target_pairs={{0,16},{1,17},{2,18},{3,19},{4,20},{5,21},{6,22},{7,23},{8,24},{9,... | collective-permute-start | bytes 2359304 | tf_op jit(solution)/shard_map/ppermute | solution.py:667
  836.2 39.0 %collective-permute-start.60 = (bf16[2,2,2,64,464]{4,3,2,1,0:T(8,128)(2,1)S(1)}, bf16[2,2,2,64,464]{4,3,2,1,0:T(8,128)(2,1)S(1)}, u32[]{:S(2)}, u32[]{:S(2)}) collective-permute-start(bf16[2,2,2,64,464]{4,3,2,1,0:T(8,128)(2,1)S(1)} %fusion.6), channel_id=1, source_target_pairs={{0,2},{1,3},{2,0},{3,1},{4,6},{5,7},{6,4},{7,5},{8,10},{9,11},{10,... | collective-permute-start | bytes 1425416 | tf_op jit(solution)/shard_map/ppermute | solution.py:667
  875.1 34.5 %collective-permute-start.58 = (bf16[128,4224]{1,0:T(8,128)(2,1)}, bf16[128,4224]{1,0:T(8,128)(2,1)S(1)}, u32[]{:S(2)}, u32[]{:S(2)}) collective-permute-start(bf16[128,4224]{1,0:T(8,128)(2,1)} %pad_maximum_fusion.11), channel_id=1, source_target_pairs={{0,1},{1,0},{2,3},{3,2},{4,5},{5,4},{6,7},{7,6},{8,9},{9,8},{10,11... | collective-permute-start | bytes 3244040 | tf_op jit(solution)/shard_map/ppermute | solution.py:667
  891.8 16.7 %collective-permute-start.62 = (bf16[128,2560]{1,0:T(8,128)(2,1)}, bf16[128,2560]{1,0:T(8,128)(2,1)}, u32[]{:S(2)}, u32[]{:S(2)}) collective-permute-start(bf16[128,2560]{1,0:T(8,128)(2,1)} %pad_maximum_fusion.22), channel_id=1, source_target_pairs={{0,8},{1,9},{2,10},{3,11},{4,12},{5,13},{6,14},{7,15},{8,0},{9,1},... | collective-permute-start | bytes 1966088 | tf_op jit(solution)/shard_map/ppermute | solution.py:667
  (131 other events, 1151.5 us)
Sparse Core Ops, SparseCore 0:
  102.1 52.3 all-gather.6
  156.3 73.6 all-gather.4
  236.6 96.4 all-gather.8
  334.8 78.8 all-gather.10
  490.0 79.4 reduce-scatter.4
  572.3 84.2 reduce-scatter.6
  659.6 70.2 reduce-scatter.8
  732.8 70.7 reduce-scatter.10
where the time goes:
time: 937 us; the launch traced here: 925 us
  waiting for transfers between devices  440 us (47%)
  Pallas kernels  269 us (29%)
  local copies, waits for them, and re-layouts  77.2 us (8%)
  starting transfers between devices  65.9 us (7%)
  other arithmetic  56.3 us (6%)
  between operations  16.3 us (2%)
    ppermute x63, waiting for transfers between devices, trade(): return lax.ppermute(value, 'seq', [(d, d ^ mask) for d in range(count)])  402 us
    pallas_call x12, Pallas kernels, product(): pl.pallas_call(kernel, grid=(outs[0][1] // tile,), in_specs=specs, out_sp...  80.1 us
    pallas_call x24, Pallas kernels, local(): pl.pallas_call(kernel, in_specs=specs, out_specs=[pl.BlockSpec(memory_spa...  72.8 us
    ppermute x63, starting transfers between devices, trade(): return lax.ppermute(value, 'seq', [(d, d ^ mask) for d in range(count)])  58.1 us
    pallas_call x4, Pallas kernels, block_call(): pl.pallas_call(kernel, grid=(chunks, width // lane), in_specs=[kinds[kind...  48.1 us
    unnamed x212, local copies, waits for them, and re-layouts  36.5 us
    pallas_call x4, Pallas kernels, weight_grad(): pl.pallas_call(kernel, grid_spec=pltpu.PrefetchScalarGridSpec(num_scalar_...  34.8 us
    all_gather x4, waiting for transfers between devices, gather_square(): lax.all_gather(paired, 'seq', axis=0, tiled=True, axis_index_groups=groups)  24.2 us
  transfers between devices with their start and end apart: 75, of which 46 were waited for; matrix products, arithmetic and copies ran while one was open for 9% of the time, Pallas kernels for 26%

commit v1 on v0

--- a/solution.py
+++ b/solution.py
@@ -713,14 +713,16 @@
             tile=512,
         )
 
-    def exchange(pieces):
+    def exchange(pieces, meet=None):
         pieces, high = list(pieces), pieces[0].shape[0]
         for j in reversed(range(len(masks))):
             keys = [k for k in range(size) if (k >> j) & 1]
             got = trade(jnp.concatenate([pieces[k] for k in keys], axis=0), masks[j])
+            if meet is not None and j == len(masks) - 1:
+                got, meet = tie(got, meet)
             for i, k in enumerate(keys):
                 pieces[k] = got[i * high : (i + 1) * high]
-        return pieces
+        return pieces if meet is None else (pieces, meet)
 
     def ordered(pieces):
         pieces = list(pieces)
@@ -823,29 +825,21 @@
             sent = lax.dynamic_index_in_dim(cube, 1 - bit, axis, keepdims=False)
             kept = lax.dynamic_index_in_dim(cube, bit, axis, keepdims=False)
             cube = kept.astype(F32) + trade(sent.astype(kind), mask).astype(F32)
-            if mask == 2:
+            if mask == 1:
                 cube, follower = tie(cube, follower)
         return cube, follower
 
-    def hand_rows(pieces, extra=None):
-        widths = [sum(p.shape[1] for p in piece) for piece in pieces]
-        joint = jnp.concatenate([p for piece in pieces for p in piece], axis=1)
+    def hand_rows(joint, extra=None, meet=None):
         mine = [
             lax.dynamic_slice_in_dim(joint, (member ^ k) * rows, rows, axis=0)
             for k in range(size)
         ]
         if extra is not None:
             mine = [jnp.concatenate([m, e], axis=1) for m, e in zip(mine, extra)]
-        by_place = exchange(mine)
-        by_member = ordered(by_place)
-        outs, start = [], 0
-        for wide in widths:
-            outs += [p[:, start : start + wide] for p in by_member]
-            start += wide
-        joined = jnp.concatenate(outs, axis=1).astype(F32)
-        if extra is None:
-            return joined
-        return joined, [p[:, start:].astype(F32) for p in by_place]
+        return exchange(mine, meet)
+
+    def columns_of(by_member, start, wide):
+        return [p[:, start : start + wide] for p in by_member]
 
     up_start, decay_start, decay_up = 5 * RANK, 10 * RANK, 10 * RANK + DRANK
     last_row = neighbour(tokens[0, -1:, :], 1)
@@ -1305,10 +1299,14 @@
     key_kept, key_got = far_split(key_pair)
     sent, main_grads, latent_more, key_got = tie(sent, main_grads, latent_more, key_got)
     main_pair = square_sum(main_grads)
-    mixed_mine, mixed_more = group_sum(kept, sent)
+    val_sum, key_sum = far_add(val_kept, val_got), far_add(key_kept, key_got)
+    mixed_mine, mixed_side = group_fold(kept, sent)
+    ff_rows, mixed_side = hand_rows(
+        jnp.concatenate([key_sum, val_sum], axis=1), meet=mixed_side
+    )
+    mixed_more = trade(mixed_side, masks[1])
     mixed_more, out_pair = tie(mixed_more, out_pair)
     out_kept, out_got = far_split(out_pair)
-    val_sum, key_sum = far_add(val_kept, val_got), far_add(key_kept, key_got)
     rest_grad, delta_grad, top_one, cols_mix, down_grad, up_grad, ddown_grad = mixes_back(
         mixed_mine,
         mixed_more,
@@ -1368,10 +1366,6 @@
     )
     main_sum = far_add(main_kept, main_got)
 
-    def column_parts(value):
-        return [value[:, c * part : (c + 1) * part] for c in range(3)]
-
-    out_cols, main_cols = column_parts(out_sum), column_parts(main_sum)
     holder = lax.div(me * rows, part)
 
     def rows_of(who):
@@ -1379,15 +1373,25 @@
         high = lax.reduce_precision(mine, 8, 7)
         return jnp.concatenate([high, mine - high], axis=1).astype(BF16)
 
-    feedforward_gradient, handed = hand_rows(
-        [[key_sum], [out_cols[1]], [val_sum]],
+    handed = hand_rows(
+        jnp.concatenate([main_sum, out_sum], axis=1),
         [rows_of(jnp.bitwise_xor(me, flips(k))) for k in range(size)],
     )
-    state_rows = handed[0]
+    state_rows = handed[0][:, 6 * part :]
     for k in range(1, size):
-        state_rows = jnp.where(holder == (member ^ k), handed[k], state_rows)
+        state_rows = jnp.where(holder == (member ^ k), handed[k][:, 6 * part :], state_rows)
+    state_rows = state_rows.astype(F32)
     initial_state_gradient = state_rows[:, :SPAN] + state_rows[:, SPAN:]
-    mixing_gradient = hand_rows([[m] for m in main_cols] + [[out_cols[2]], [out_cols[0]]])
+    by_member, ff_member = ordered(handed), ordered(ff_rows)
+    mixing_gradient = jnp.concatenate(
+        [p for c in (0, 1, 2, 5, 3) for p in columns_of(by_member, c * part, part)], axis=1
+    ).astype(F32)
+    feedforward_gradient = jnp.concatenate(
+        columns_of(ff_member, 0, ff_part)
+        + columns_of(by_member, 4 * part, part)
+        + columns_of(ff_member, ff_part, ff_part),
+        axis=1,
+    ).astype(F32)
 
     vec_at = decay_up + 12
     lowrank_gradient = jnp.concatenate(

time: 937 us -> 939 us (level)
    unnamed x212 -> x227, local copies, waits for them, and re-layouts: 36.5 us -> 42.7 us
  transfers between devices with their start and end apart: 75 -> 75, of which waited for: 46 -> 49; matrix products, arithmetic and copies ran while one was open for 9% -> 9% of each run, Pallas kernels for 26% -> 26%
where the time goes in v1:
time: 939 us; the launch traced here: 927 us
  waiting for transfers between devices  440 us (47%)
  Pallas kernels  269 us (29%)
  local copies, waits for them, and re-layouts  82.9 us (9%)
  starting transfers between devices  63.4 us (7%)
  other arithmetic  55.8 us (6%)
  between operations  16.3 us (2%)
    ppermute x63, waiting for transfers between devices, trade(): return lax.ppermute(value, 'seq', [(d, d ^ mask) for d in range(count)])  409 us
    pallas_call x12, Pallas kernels, product(): pl.pallas_call(kernel, grid=(outs[0][1] // tile,), in_specs=specs, out_sp...  80.1 us
    pallas_call x24, Pallas kernels, local(): pl.pallas_call(kernel, in_specs=specs, out_specs=[pl.BlockSpec(memory_spa...  72.8 us
    ppermute x63, starting transfers between devices, trade(): return lax.ppermute(value, 'seq', [(d, d ^ mask) for d in range(count)])  55.9 us
    pallas_call x4, Pallas kernels, block_call(): pl.pallas_call(kernel, grid=(chunks, width // lane), in_specs=[kinds[kind...  48.1 us
    unnamed x227, local copies, waits for them, and re-layouts  42.7 us
    pallas_call x4, Pallas kernels, weight_grad(): pl.pallas_call(kernel, grid_spec=pltpu.PrefetchScalarGridSpec(num_scalar_...  34.8 us
    all_gather x4, waiting for transfers between devices, gather_square(): lax.all_gather(paired, 'seq', axis=0, tiled=True, axis_index_groups=groups)  24.2 us
  transfers between devices with their start and end apart: 75, of which 49 were waited for; matrix products, arithmetic and copies ran while one was open for 9% of the time, Pallas kernels for 26%

profile of v1, /device:TPU:0, one launch (start us, length us, event | category | flops | bytes accessed | tf_op | source)
XLA Modules:
  0.0 927.3 jit_solution(6387528985843947491)
XLA Ops:
  25.1 13.4 %collective-permute-done.4 = f32[2,64,144]{2,1,0:T(8,128)S(1)} collective-permute-done((f32[2,64,144]{2,1,0:T(8,128)S(1)}, f32[2,64,144]{2,1,0:T(8,128)S(1)}, u32[]{:S(2)}, u32[]{:S(2)}) %collective-permute-start.4) | collective-permute-done | bytes 73760 | tf_op jit(solution)/shard_map/ppermute | solution.py:667
  52.9 9.9 %collective-permute-done.8 = f32[2,2,2,64,144]{4,3,2,1,0:T(8,128)S(1)} collective-permute-done((f32[2,2,2,64,144]{4,3,2,1,0:T(8,128)S(1)}, f32[2,2,2,64,144]{4,3,2,1,0:T(8,128)S(1)}, u32[]{:S(2)}, u32[]{:S(2)}) %collective-permute-start.8) | collective-permute-done | bytes 294944 | tf_op jit(solution)/shard_map/ppermute | solution.py:667
  76.8 24.0 %collective-permute-done.15 = bf16[256,1024]{1,0:T(8,128)(2,1)S(1)} collective-permute-done((bf16[256,1024]{1,0:T(8,128)(2,1)S(1)}, bf16[256,1024]{1,0:T(8,128)(2,1)S(1)}, u32[]{:S(2)}, u32[]{:S(2)}) %collective-permute-start.15) | collective-permute-done | bytes 524320 | tf_op jit(solution)/shard_map/ppermute | solution.py:667
  110.1 16.4 %shard_map.137 = (bf16[512,2048]{1,0:T(8,128)(2,1)}, bf16[512,2048]{1,0:T(8,128)(2,1)}, bf16[512,2048]{1,0:T(8,128)(2,1)}, bf16[512,2048]{1,0:T(8,128)(2,1)}, bf...) custom-call(s32[4]{0:T(128)} %add_convert_fusion.4.open_ref, ...), custom_call_target="tpu_custom_call" | custom-call | tf_op jit(solution)/shard_map/pallas_call | solution.py:386
  126.5 12.2 %collective-permute-done.16 = bf16[256,1536]{1,0:T(8,128)(2,1)} collective-permute-done((bf16[256,1536]{1,0:T(8,128)(2,1)S(1)}, bf16[256,1536]{1,0:T(8,128)(2,1)}, u32[]{:S(2)}, u32[]{:S(2)}) %collective-permute-start.16) | collective-permute-done | bytes 786464 | tf_op jit(solution)/shard_map/ppermute | solution.py:667
  142.4 23.9 %collective-permute-done.17 = bf16[128,4096]{1,0:T(8,128)(2,1)S(1)} collective-permute-done((bf16[128,4096]{1,0:T(8,128)(2,1)S(1)}, bf16[128,4096]{1,0:T(8,128)(2,1)S(1)}, u32[]{:S(2)}, u32[]{:S(2)}) %collective-permute-start.17) | collective-permute-done | bytes 1048608 | tf_op jit(solution)/shard_map/ppermute | solution.py:667
  211.3 22.2 %collective-permute-done.20 = bf16[256,2304]{1,0:T(8,128)(2,1)} collective-permute-done((bf16[256,2304]{1,0:T(8,128)(2,1)}, bf16[256,2304]{1,0:T(8,128)(2,1)}, u32[]{:S(2)}, u32[]{:S(2)}) %collective-permute-start.20) | collective-permute-done | bytes 1179680 | tf_op jit(solution)/shard_map/ppermute | solution.py:667
  263.7 14.3 %shard_map.146 = (f32[512,512]{1,0:T(8,128)S(1)}, bf16[512,512]{1,0:T(8,128)(2,1)S(1)}) custom-call(f32[512,512]{1,0:T(8,128)S(1)} %copy-done.9, f32[512,512]{1,0:T(8,128)S(1)} %copy-done.7, f32[512,512]{1,0:T(8,128)S(1)} %copy-done.8, f32[512,512]{1,0:T(8,128)} %shard_map.140.w_ref, f32[512,512]{1,0:T(8,128)} %get-tuple-element.175.g_ref, ...), custom_call_target="tpu_custom_call" | custom-call | tf_op jit(solution)/shard_map/pallas_call | solution.py:222
  279.7 16.6 %collective-permute-done.23 = bf16[256,1792]{1,0:T(8,128)(2,1)} collective-permute-done((bf16[256,1792]{1,0:T(8,128)(2,1)S(1)}, bf16[256,1792]{1,0:T(8,128)(2,1)}, u32[]{:S(2)}, u32[]{:S(2)}) %collective-permute-start.23) | collective-permute-done | bytes 917536 | tf_op jit(solution)/shard_map/ppermute | solution.py:667
  311.0 14.2 %collective-permute-done.25.refs_2_ = bf16[128,2048]{1,0:T(8,128)(2,1)S(1)} collective-permute-done((bf16[128,2048]{1,0:T(8,128)(2,1)}, bf16[128,2048]{1,0:T(8,128)(2,1)S(1)}, u32[]{:S(2)}, u32[]{:S(2)}) %collective-permute-start.25) | collective-permute-done | bytes 524320 | tf_op jit(solution)/shard_map/ppermute | solution.py:667
  341.9 12.7 %collective-permute-done.27.refs_1_ = bf16[128,2048]{1,0:T(8,128)(2,1)S(1)} collective-permute-done((bf16[128,2048]{1,0:T(8,128)(2,1)S(1)}, bf16[128,2048]{1,0:T(8,128)(2,1)S(1)}, u32[]{:S(2)}, u32[]{:S(2)}) %collective-permute-start.27) | collective-permute-done | bytes 524320 | tf_op jit(solution)/shard_map/ppermute | solution.py:667
  354.8 10.1 %collective-permute-done.29.refs_1_ = bf16[128,2048]{1,0:T(8,128)(2,1)S(1)} collective-permute-done((bf16[128,2048]{1,0:T(8,128)(2,1)S(1)}, bf16[128,2048]{1,0:T(8,128)(2,1)S(1)}, u32[]{:S(2)}, u32[]{:S(2)}) %collective-permute-start.29) | collective-permute-done | bytes 524320 | tf_op jit(solution)/shard_map/ppermute | solution.py:667
  380.6 9.0 shard_map.152
  389.6 24.1 %all-gather.11.cloned.1.call-done.refs_1_ = bf16[2048,1792]{1,0:T(8,128)(2,1)} async-done(((bf16[512,1792]{1,0:T(8,128)(2,1)}), bf16[2048,1792]{1,0:T(8,128)(2,1)}) %all-gather.11.cloned.1.call-update) | async-done | bytes 7340048 | tf_op jit(solution)/shard_map/all_gather | solution.py:775
  437.5 12.2 %collective-permute-done.32.more_ref = bf16[128,2048]{1,0:T(8,128)(2,1)S(1)} collective-permute-done((bf16[128,2048]{1,0:T(8,128)(2,1)}, bf16[128,2048]{1,0:T(8,128)(2,1)S(1)}, u32[]{:S(2)}, u32[]{:S(2)}) %collective-permute-start.32) | collective-permute-done | bytes 524320 | tf_op jit(solution)/shard_map/ppermute | solution.py:667
  457.5 12.0 %collective-permute-done.35.refs_1_ = bf16[128,2048]{1,0:T(8,128)(2,1)S(1)} collective-permute-done((bf16[128,2048]{1,0:T(8,128)(2,1)}, bf16[128,2048]{1,0:T(8,128)(2,1)S(1)}, u32[]{:S(2)}, u32[]{:S(2)}) %collective-permute-start.35) | collective-permute-done | bytes 524320 | tf_op jit(solution)/shard_map/ppermute | solution.py:667
  490.1 9.0 shard_map.160.refs_1_.refs_0_
  508.6 8.3 shard_map.162
  532.9 8.8 collective-permute-done.40.refs_1_
  541.7 10.9 %collective-permute-done.42.refs_3_ = bf16[128,2048]{1,0:T(8,128)(2,1)S(1)} collective-permute-done((bf16[128,2048]{1,0:T(8,128)(2,1)}, bf16[128,2048]{1,0:T(8,128)(2,1)S(1)}, u32[]{:S(2)}, u32[]{:S(2)}) %collective-permute-start.42) | collective-permute-done | bytes 524320 | tf_op jit(solution)/shard_map/ppermute | solution.py:667
  569.2 11.3 %collective-permute-done.44.refs_1_ = bf16[128,2048]{1,0:T(8,128)(2,1)S(1)} collective-permute-done((bf16[128,2048]{1,0:T(8,128)(2,1)}, bf16[128,2048]{1,0:T(8,128)(2,1)S(1)}, u32[]{:S(2)}, u32[]{:S(2)}) %collective-permute-start.44) | collective-permute-done | bytes 524320 | tf_op jit(solution)/shard_map/ppermute | solution.py:667
  597.9 12.2 %shard_map.170 = (bf16[512,512]{1,0:T(8,128)(2,1)S(1)}, f32[512,512]{1,0:T(8,128)S(1)}, f32[4,72,512]{2,1,0:T(8,128)S(1)}) custom-call(f32[512,512]{1,0:T(8,128)S(1)} %copy-done.15, f32[512,512]{1,0:T(8,128)S(1)} %copy-done.16, f32[512,512]{1,0:T(8,128)S(1)} %copy-done.29, f32[512,512]{1,0:T(8,128)} %get-tuple-element.166.r_ref, ...), custom_call_target="tpu_custom_call" | custom-call | tf_op jit(solution)/shard_map/pallas_call | solution.py:222
  642.0 9.4 %shard_map.175 = bf16[8,256,1536]{2,1,0:T(8,128)(2,1)} custom-call(s32[8]{0:T(128)S(1)} %iota.14._, bf16[512,2048]{1,0:T(8,128)(2,1)S(1)} %copy-done.4, bf16[512,512]{1,0:T(8,128)(2,1)S(1)} %copy-done.27, bf16[512,2048]{1,0:T(8,128)(2,1)S(1)} %copy-done.2, bf16[512,512]{1,0:T(8,128)(2,1)S(1)} %copy-done.14, ...), custom_call_target="tpu_custom_call" | custom-call | tf_op jit(solution)/shard_map/pallas_call | solution.py:248
  661.5 14.8 %shard_map.176 = (bf16[512,512]{1,0:T(8,128)(2,1)S(1)}, bf16[512,512]{1,0:T(8,128)(2,1)S(1)}, bf16[512,512]{1,0:T(8,128)(2,1)S(1)}, bf16[512,512]{1,0:T(8,128)(2,1)S(1)}, f32[4,8,512]{2,1,0:T(8,128)S(1)}) custom-call(f32[512,512]{1,0:T(8,128)S(1)} %copy-done.10, f32[512,512]{1,0:T(8,128)S(1)} %copy-done.7, f32[512,512]{1,0:T(8,128)} %get-tuple-element.173.v_ref, ...), custom_call_target="tpu_custom_call" | custom-call | tf_op jit(solution)/shard_map/pallas_call | solution.py:222
  686.6 9.4 %shard_map.178 = bf16[8,256,1536]{2,1,0:T(8,128)(2,1)} custom-call(s32[8]{0:T(128)S(1)} %iota.15._, bf16[512,2048]{1,0:T(8,128)(2,1)S(1)} %copy-done.11, bf16[512,512]{1,0:T(8,128)(2,1)S(1)} %get-tuple-element.251.refs_0_.refs_1_, bf16[512,2048]{1,0:T(8,128)(2,1)S(1)} %copy-done.12, bf16[512,512]{1,0:T(8,128)(2,1)S(1)} %get-tuple-element.252.refs_2_.refs_3_, ...), custom_call_target="tpu_custom_call" | custom-call | tf_op jit(solution)/shard_map/pallas_call | solution.py:248
  696.1 11.1 %shard_map.177 = (f32[1024,2048]{1,0:T(8,128)}, bf16[1024,2048]{1,0:T(8,128)(2,1)}) custom-call(bf16[512,512]{1,0:T(8,128)(2,1)} %copy-done.20, bf16[2048,1024]{1,0:T(8,128)(2,1)} %all-gather.7.cloned.1.call-done.refs_1_.refs_3_, bf16[512,512]{1,0:T(8,128)(2,1)} %copy-done.21, bf16[2048,1024]{1,0:T(8,128)(2,1)} %all-gather.7.cloned.1.call-done.refs_1_.refs_3_, ...), custom_call_target="tpu_custom_call" | custom-call | tf_op jit(solution)/shard_map/pallas_call | solution.py:428
  723.1 11.4 %collective-permute-done.54 = bf16[128,3584]{1,0:T(8,128)(2,1)S(1)} collective-permute-done((bf16[128,3584]{1,0:T(8,128)(2,1)S(1)}, bf16[128,3584]{1,0:T(8,128)(2,1)S(1)}, u32[]{:S(2)}, u32[]{:S(2)}) %collective-permute-start.54) | collective-permute-done | bytes 917536 | tf_op jit(solution)/shard_map/ppermute | solution.py:667
  744.4 37.8 %collective-permute-done.55.got_ref = bf16[512,2048]{1,0:T(8,128)(2,1)} collective-permute-done((bf16[512,2048]{1,0:T(8,128)(2,1)}, bf16[512,2048]{1,0:T(8,128)(2,1)}, u32[]{:S(2)}, u32[]{:S(2)}) %collective-permute-start.55) | collective-permute-done | bytes 2097184 | tf_op jit(solution)/shard_map/ppermute | solution.py:667
  787.0 12.2 %shard_map.182 = (f32[128,2048]{1,0:T(8,128)}, f32[128,2048]{1,0:T(8,128)}, f32[8,2048]{1,0:T(8,128)}, f32[8,2048]{1,0:T(8,128)}, f32[2048,160]{1,0:T(8,128)}, /*index=5*/f32[2048,160]{1,0:T(8,128)}, f32[2048,64]{1,0:T(8,128)}) custom-call(f32[512,2048]{1,0:T(8,128)} %get-tuple-element.262.kept_ref, bf16[512,2048]{1,0:T(8,128)(2,1)} %collective-permute-done.55.got_ref, ...), custom_call_target="tpu_custom_call" | custom-call | tf_op jit(solution)/shard_map/pallas_call | solution.py:597
  803.2 17.4 %collective-permute-done.56 = bf16[256,1536]{1,0:T(8,128)(2,1)S(1)} collective-permute-done((bf16[256,1536]{1,0:T(8,128)(2,1)}, bf16[256,1536]{1,0:T(8,128)(2,1)S(1)}, u32[]{:S(2)}, u32[]{:S(2)}) %collective-permute-start.56) | collective-permute-done | bytes 786464 | tf_op jit(solution)/shard_map/ppermute | solution.py:667
  834.4 35.1 %collective-permute-done.59 = bf16[256,1536]{1,0:T(8,128)(2,1)S(1)} collective-permute-done((bf16[256,1536]{1,0:T(8,128)(2,1)S(1)}, bf16[256,1536]{1,0:T(8,128)(2,1)S(1)}, u32[]{:S(2)}, u32[]{:S(2)}) %collective-permute-start.59) | collective-permute-done | bytes 786464 | tf_op jit(solution)/shard_map/ppermute | solution.py:667
  873.9 10.9 %collective-permute-done.62 = bf16[2,2,2,64,464]{4,3,2,1,0:T(8,128)(2,1)} collective-permute-done((bf16[2,2,2,64,464]{4,3,2,1,0:T(8,128)(2,1)}, bf16[2,2,2,64,464]{4,3,2,1,0:T(8,128)(2,1)}, u32[]{:S(2)}, u32[]{:S(2)}) %collective-permute-start.62) | collective-permute-done | bytes 475168 | tf_op jit(solution)/shard_map/ppermute | solution.py:667
  (561 shorter events, 433.7 us)
Async XLA Ops:
  7.2 164.4 %all-gather.7.cloned.1.call-start = ((), (), s32[]{:S(2)}) async-start(), calls=%async_computation.5 | async-start | bytes 5242880 | tf_op jit(solution)/shard_map/all_gather | solution.py:775
  18.7 44.4 %collective-permute-start.13 = (bf16[144,2048]{1,0:T(8,128)(2,1)S(1)}, bf16[144,2048]{1,0:T(8,128)(2,1)S(1)}, u32[]{:S(2)}, u32[]{:S(2)}) collective-permute-start(bf16[144,2048]{1,0:T(8,128)(2,1)S(1)} %shard_map.135.refs_0_), channel_id=1, source_target_pairs={{0,8},{1,9},{2,10},{3,11},{4,12},{5,13},{6,14},{7,15},{8,0},{9,1},... | collective-permute-start | bytes 1769480 | tf_op jit(solution)/shard_map/ppermute | solution.py:667
  22.9 15.6 %collective-permute-start.4 = (f32[2,64,144]{2,1,0:T(8,128)S(1)}, f32[2,64,144]{2,1,0:T(8,128)S(1)}, u32[]{:S(2)}, u32[]{:S(2)}) collective-permute-start(f32[2,64,144]{2,1,0:T(8,128)S(1)} %pad_maximum_fusion.32), channel_id=1, source_target_pairs={{0,8},{1,9},{2,10},{3,11},{4,12},{5,13},{6,14},{7,15},{8,0},{9,1},... | collective-permute-start | bytes 221192 | tf_op jit(solution)/shard_map/ppermute | solution.py:667
  24.7 15.9 %collective-permute-start.2 = (bf16[2,64,384]{2,1,0:T(8,128)(2,1)S(1)}, bf16[2,64,384]{2,1,0:T(8,128)(2,1)S(1)}, u32[]{:S(2)}, u32[]{:S(2)}) collective-permute-start(bf16[2,64,384]{2,1,0:T(8,128)(2,1)S(1)} %pad_maximum_fusion.35), channel_id=1, source_target_pairs={{0,8},{1,9},{2,10},{3,11},{4,12},{5,13},{6,14},{7,15},{8,0},{9,1},... | collective-permute-start | bytes 294920 | tf_op jit(solution)/shard_map/ppermute | solution.py:667
  40.9 22.8 %collective-permute-start.5 = (bf16[128,2560]{1,0:T(8,128)(2,1)S(1)}, bf16[128,2560]{1,0:T(8,128)(2,1)S(1)}, u32[]{:S(2)}, u32[]{:S(2)}) collective-permute-start(bf16[128,2560]{1,0:T(8,128)(2,1)S(1)} %pad_maximum_fusion.20), channel_id=1, source_target_pairs={{0,8},{1,9},{2,10},{3,11},{4,12},{5,13},{6,14},{7,15},{8,0},{9,1},... | collective-permute-start | bytes 1966088 | tf_op jit(solution)/shard_map/ppermute | solution.py:667
  51.3 17.5 %collective-permute-start.11 = (bf16[2,2,2,64,384]{4,3,2,1,0:T(8,128)(2,1)S(1)}, bf16[2,2,2,64,384]{4,3,2,1,0:T(8,128)(2,1)S(1)}, u32[]{:S(2)}, u32[]{:S(2)}) collective-permute-start(bf16[2,2,2,64,384]{4,3,2,1,0:T(8,128)(2,1)S(1)} %pad_maximum_fusion.27), channel_id=1, source_target_pairs={{0,2},{1,3},{2,0},{3,1},{4,6},{5,7},{6,4},{7,5},{8,10},{9,11},{10,... | collective-permute-start | bytes 1179656 | tf_op jit(solution)/shard_map/ppermute | solution.py:667
  74.6 26.2 %collective-permute-start.15 = (bf16[256,1024]{1,0:T(8,128)(2,1)S(1)}, bf16[256,1024]{1,0:T(8,128)(2,1)S(1)}, u32[]{:S(2)}, u32[]{:S(2)}) collective-permute-start(bf16[256,1024]{1,0:T(8,128)(2,1)S(1)} %slice.303), channel_id=1, source_target_pairs={{0,16},{1,17},{2,18},{3,19},{4,20},{5,21},{6,22},{7,23},{8,24},{9,... | collective-permute-start | bytes 1572872 | tf_op jit(solution)/shard_map/ppermute | solution.py:667
  101.9 153.9 %all-gather.5.cloned.1.call-start = ((), (), s32[]{:S(2)}) async-start(), calls=%async_computation.4 | async-start | bytes 7864320 | tf_op jit(solution)/shard_map/all_gather | solution.py:775
  102.0 36.7 %collective-permute-start.16 = (bf16[256,1536]{1,0:T(8,128)(2,1)S(1)}, bf16[256,1536]{1,0:T(8,128)(2,1)}, u32[]{:S(2)}, u32[]{:S(2)}) collective-permute-start(bf16[256,1536]{1,0:T(8,128)(2,1)S(1)} %slice.304), channel_id=1, source_target_pairs={{0,16},{1,17},{2,18},{3,19},{4,20},{5,21},{6,22},{7,23},{8,24},{9,... | collective-permute-start | bytes 2359304 | tf_op jit(solution)/shard_map/ppermute | solution.py:667
  141.2 231.9 %all-gather.9.cloned.1.call-start = ((), (), s32[]{:S(2)}) async-start(), calls=%async_computation.6 | async-start | bytes 11796480 | tf_op jit(solution)/shard_map/all_gather | solution.py:775
  142.4 24.0 %collective-permute-start.17 = (bf16[128,4096]{1,0:T(8,128)(2,1)S(1)}, bf16[128,4096]{1,0:T(8,128)(2,1)S(1)}, u32[]{:S(2)}, u32[]{:S(2)}) collective-permute-start(bf16[128,4096]{1,0:T(8,128)(2,1)S(1)} %maximum_maximum_fusion), channel_id=1, source_target_pairs={{0,8},{1,9},{2,10},{3,11},{4,12},{5,13},{6,14},{7,15},{8,0},{9,1},... | collective-permute-start | bytes 3145736 | tf_op jit(solution)/shard_map/ppermute | solution.py:667
  179.3 54.2 %collective-permute-start.20 = (bf16[256,2304]{1,0:T(8,128)(2,1)}, bf16[256,2304]{1,0:T(8,128)(2,1)}, u32[]{:S(2)}, u32[]{:S(2)}) collective-permute-start(bf16[256,2304]{1,0:T(8,128)(2,1)} %slice.312), channel_id=1, source_target_pairs={{0,16},{1,17},{2,18},{3,19},{4,20},{5,21},{6,22},{7,23},{8,24},{9,... | collective-permute-start | bytes 3538952 | tf_op jit(solution)/shard_map/ppermute | solution.py:667
  236.5 177.2 %all-gather.11.cloned.1.call-start = ((), (), s32[]{:S(2)}) async-start(), calls=%async_computation.7 | async-start | bytes 9175040 | tf_op jit(solution)/shard_map/all_gather | solution.py:775
  255.3 41.0 %collective-permute-start.23 = (bf16[256,1792]{1,0:T(8,128)(2,1)S(1)}, bf16[256,1792]{1,0:T(8,128)(2,1)}, u32[]{:S(2)}, u32[]{:S(2)}) collective-permute-start(bf16[256,1792]{1,0:T(8,128)(2,1)S(1)} %slice.314), channel_id=1, source_target_pairs={{0,16},{1,17},{2,18},{3,19},{4,20},{5,21},{6,22},{7,23},{8,24},{9,... | collective-permute-start | bytes 2752520 | tf_op jit(solution)/shard_map/ppermute | solution.py:667
  299.1 284.7 %reduce-scatter.5.cloned.1.call-start = ((), (), s32[]{:S(2)}) async-start(), calls=%async_computation.8 | async-start | bytes 9175040 | tf_op jit(solution)/shard_map/reduce_scatter | solution.py:785
  336.3 18.3 %collective-permute-start.27 = (bf16[128,2048]{1,0:T(8,128)(2,1)S(1)}, bf16[128,2048]{1,0:T(8,128)(2,1)S(1)}, u32[]{:S(2)}, u32[]{:S(2)}) collective-permute-start(bf16[128,2048]{1,0:T(8,128)(2,1)S(1)} %get-tuple-element.391.refs_0_), channel_id=1, source_target_pairs={{0,8},{1,9},{2,10},{3,11},{4,12},{5,13},{6,14},{7,15},{8,0},{9,1},... | collective-permute-start | bytes 1572872 | tf_op jit(solution)/shard_map/ppermute | solution.py:667
  341.8 23.1 %collective-permute-start.29 = (bf16[128,2048]{1,0:T(8,128)(2,1)S(1)}, bf16[128,2048]{1,0:T(8,128)(2,1)S(1)}, u32[]{:S(2)}, u32[]{:S(2)}) collective-permute-start(bf16[128,2048]{1,0:T(8,128)(2,1)S(1)} %get-tuple-element.390.refs_0_), channel_id=1, source_target_pairs={{0,8},{1,9},{2,10},{3,11},{4,12},{5,13},{6,14},{7,15},{8,0},{9,1},... | collective-permute-start | bytes 1572872 | tf_op jit(solution)/shard_map/ppermute | solution.py:667
  454.5 15.0 %collective-permute-start.35 = (bf16[128,2048]{1,0:T(8,128)(2,1)}, bf16[128,2048]{1,0:T(8,128)(2,1)S(1)}, u32[]{:S(2)}, u32[]{:S(2)}) collective-permute-start(bf16[128,2048]{1,0:T(8,128)(2,1)} %get-tuple-element.210.refs_0_), channel_id=1, source_target_pairs={{0,8},{1,9},{2,10},{3,11},{4,12},{5,13},{6,14},{7,15},{8,0},{9,1},... | collective-permute-start | bytes 1572872 | tf_op jit(solution)/shard_map/ppermute | solution.py:667
  456.9 16.9 %collective-permute-start.37 = (bf16[256,512]{1,0:T(8,128)(2,1)S(1)}, bf16[256,512]{1,0:T(8,128)(2,1)S(1)}, u32[]{:S(2)}, u32[]{:S(2)}) collective-permute-start(bf16[256,512]{1,0:T(8,128)(2,1)S(1)} %concatenate.199), channel_id=1, source_target_pairs={{0,8},{1,9},{2,10},{3,11},{4,12},{5,13},{6,14},{7,15},{8,0},{9,1},... | collective-permute-start | bytes 786440 | tf_op jit(solution)/shard_map/ppermute | solution.py:667
  490.0 166.7 %reduce-scatter.7.cloned.1.call-start = ((), (), s32[]{:S(2)}) async-start(), calls=%async_computation.9 | async-start | bytes 9175040 | tf_op jit(solution)/shard_map/reduce_scatter | solution.py:785
  508.6 273.6 %reduce-scatter.9.cloned.1.call-start = ((), (), s32[]{:S(2)}) async-start(), calls=%async_computation.10 | async-start | bytes 7864320 | tf_op jit(solution)/shard_map/reduce_scatter | solution.py:785
  532.5 20.1 %collective-permute-start.42 = (bf16[128,2048]{1,0:T(8,128)(2,1)}, bf16[128,2048]{1,0:T(8,128)(2,1)S(1)}, u32[]{:S(2)}, u32[]{:S(2)}) collective-permute-start(bf16[128,2048]{1,0:T(8,128)(2,1)} %get-tuple-element.223), channel_id=1, source_target_pairs={{0,8},{1,9},{2,10},{3,11},{4,12},{5,13},{6,14},{7,15},{8,0},{9,1},... | collective-permute-start | bytes 1572872 | tf_op jit(solution)/shard_map/ppermute | solution.py:667
  585.9 43.5 %collective-permute-start.47 = (bf16[256,1792]{1,0:T(8,128)(2,1)}, bf16[256,1792]{1,0:T(8,128)(2,1)}, u32[]{:S(2)}, u32[]{:S(2)}) collective-permute-start(bf16[256,1792]{1,0:T(8,128)(2,1)} %constant_dynamic-slice_fusion.3), channel_id=1, source_target_pairs={{0,16},{1,17},{2,18},{3,19},{4,20},{5,21},{6,22},{7,23},{8,24},{9,... | collective-permute-start | bytes 2752520 | tf_op jit(solution)/shard_map/ppermute | solution.py:667
  654.2 149.0 %reduce-scatter.11.cloned.1.call-start = ((), (), s32[]{:S(2)}) async-start(), calls=%async_computation.11 | async-start | bytes 7864320 | tf_op jit(solution)/shard_map/reduce_scatter | solution.py:785
  658.9 48.3 %collective-permute-start.52 = (bf16[256,1792]{1,0:T(8,128)(2,1)}, bf16[256,1792]{1,0:T(8,128)(2,1)}, u32[]{:S(2)}, u32[]{:S(2)}) collective-permute-start(bf16[256,1792]{1,0:T(8,128)(2,1)} %constant_dynamic-slice_fusion.2), channel_id=1, source_target_pairs={{0,16},{1,17},{2,18},{3,19},{4,20},{5,21},{6,22},{7,23},{8,24},{9,... | collective-permute-start | bytes 2752520 | tf_op jit(solution)/shard_map/ppermute | solution.py:667
  683.2 24.0 %collective-permute-start.51 = (bf16[128,64]{1,0:T(8,128)(2,1)}, bf16[128,64]{1,0:T(8,128)(2,1)S(1)}, u32[]{:S(2)}, u32[]{:S(2)}) collective-permute-start(bf16[128,64]{1,0:T(8,128)(2,1)} %get-tuple-element.259), channel_id=1, source_target_pairs={{0,8},{1,9},{2,10},{3,11},{4,12},{5,13},{6,14},{7,15},{8,0},{9,1},... | collective-permute-start | bytes 49160 | tf_op jit(solution)/shard_map/ppermute | solution.py:667
  711.5 23.0 %collective-permute-start.54 = (bf16[128,3584]{1,0:T(8,128)(2,1)S(1)}, bf16[128,3584]{1,0:T(8,128)(2,1)S(1)}, u32[]{:S(2)}, u32[]{:S(2)}) collective-permute-start(bf16[128,3584]{1,0:T(8,128)(2,1)S(1)} %pad_maximum_fusion.15), channel_id=1, source_target_pairs={{0,8},{1,9},{2,10},{3,11},{4,12},{5,13},{6,14},{7,15},{8,0},{9,1},... | collective-permute-start | bytes 2752520 | tf_op jit(solution)/shard_map/ppermute | solution.py:667
  734.5 47.6 %collective-permute-start.55 = (bf16[512,2048]{1,0:T(8,128)(2,1)}, bf16[512,2048]{1,0:T(8,128)(2,1)}, u32[]{:S(2)}, u32[]{:S(2)}) collective-permute-start(bf16[512,2048]{1,0:T(8,128)(2,1)} %get-tuple-element.266), channel_id=1, source_target_pairs={{0,8},{1,9},{2,10},{3,11},{4,12},{5,13},{6,14},{7,15},{8,0},{9,1},... | collective-permute-start | bytes 6291464 | tf_op jit(solution)/shard_map/ppermute | solution.py:667
  784.5 36.1 %collective-permute-start.56 = (bf16[256,1536]{1,0:T(8,128)(2,1)}, bf16[256,1536]{1,0:T(8,128)(2,1)S(1)}, u32[]{:S(2)}, u32[]{:S(2)}) collective-permute-start(bf16[256,1536]{1,0:T(8,128)(2,1)} %constant_dynamic-slice_fusion.1), channel_id=1, source_target_pairs={{0,16},{1,17},{2,18},{3,19},{4,20},{5,21},{6,22},{7,23},{8,24},{9,... | collective-permute-start | bytes 2359304 | tf_op jit(solution)/shard_map/ppermute | solution.py:667
  799.1 21.5 %collective-permute-start.57 = (f32[8,2048]{1,0:T(8,128)}, f32[8,2048]{1,0:T(8,128)S(1)}, u32[]{:S(2)}, u32[]{:S(2)}) collective-permute-start(f32[8,2048]{1,0:T(8,128)} %get-tuple-element.281), channel_id=1, source_target_pairs={{1,0},{2,1},{3,2},{4,3},{5,4},{6,5},{7,6},{8,7},{9,8},{10,9},{11,1... | collective-permute-start | bytes 196616 | tf_op jit(solution)/shard_map/ppermute | solution.py:738
  832.5 37.0 %collective-permute-start.59 = (bf16[256,1536]{1,0:T(8,128)(2,1)S(1)}, bf16[256,1536]{1,0:T(8,128)(2,1)S(1)}, u32[]{:S(2)}, u32[]{:S(2)}) collective-permute-start(bf16[256,1536]{1,0:T(8,128)(2,1)S(1)} %constant_dynamic-slice_fusion), channel_id=1, source_target_pairs={{0,16},{1,17},{2,18},{3,19},{4,20},{5,21},{6,22},{7,23},{8,24},{9,... | collective-permute-start | bytes 2359304 | tf_op jit(solution)/shard_map/ppermute | solution.py:667
  873.9 20.5 %collective-permute-start.60 = (bf16[128,3200]{1,0:T(8,128)(2,1)}, bf16[128,3200]{1,0:T(8,128)(2,1)}, u32[]{:S(2)}, u32[]{:S(2)}) collective-permute-start(bf16[128,3200]{1,0:T(8,128)(2,1)} %pad_maximum_fusion.17), channel_id=1, source_target_pairs={{0,8},{1,9},{2,10},{3,11},{4,12},{5,13},{6,14},{7,15},{8,0},{9,1},... | collective-permute-start | bytes 2457608 | tf_op jit(solution)/shard_map/ppermute | solution.py:667
  (140 other events, 1265.4 us)
Sparse Core Ops, SparseCore 0:
  102.1 52.3 all-gather.6
  156.3 73.7 all-gather.4
  236.6 96.4 all-gather.8
  334.8 78.8 all-gather.10
  490.1 79.4 reduce-scatter.4
  572.5 84.2 reduce-scatter.6
  659.7 70.2 reduce-scatter.8
  733.0 70.1 reduce-scatter.10

commit v2 on v1

--- a/solution.py
+++ b/solution.py
@@ -819,15 +819,13 @@
         back = [place_axes.index(a) for a in range(len(place_axes))]
         return cube.transpose(*back, len(back), len(back) + 1)
 
-    def cube_sum(cube, kind, follower):
+    def cube_sum(cube, kind):
         for axis, mask in reversed(list(enumerate(reversed(all_masks)))):
             bit = bit_of(me, mask)
             sent = lax.dynamic_index_in_dim(cube, 1 - bit, axis, keepdims=False)
             kept = lax.dynamic_index_in_dim(cube, bit, axis, keepdims=False)
             cube = kept.astype(F32) + trade(sent.astype(kind), mask).astype(F32)
-            if mask == 1:
-                cube, follower = tie(cube, follower)
-        return cube, follower
+        return cube
 
     def hand_rows(joint, extra=None, meet=None):
         mine = [
@@ -1305,8 +1303,8 @@
         jnp.concatenate([key_sum, val_sum], axis=1), meet=mixed_side
     )
     mixed_more = trade(mixed_side, masks[1])
-    mixed_more, out_pair = tie(mixed_more, out_pair)
     out_kept, out_got = far_split(out_pair)
+    mixed_more, out_got = tie(mixed_more, out_got)
     rest_grad, delta_grad, top_one, cols_mix, down_grad, up_grad, ddown_grad = mixes_back(
         mixed_mine,
         mixed_more,
@@ -1322,7 +1320,9 @@
         w_ddown,
         vec,
     )
-    rest_grad, main_pair, out_got = tie(rest_grad, main_pair, out_got)
+    rest_grad, main_pair = tie(rest_grad, main_pair)
+    main_kept, main_got = far_split(main_pair)
+    rest_grad, main_got = tie(rest_grad, main_got)
     out_sum = far_add(out_kept, out_got)
 
     def norm_one_back(last, rest, shifted, arrived, normal, scale, middle, vec):
@@ -1344,26 +1344,25 @@
         vec,
         scalar=last_flag,
     )
-    main_kept, main_got = far_split(main_pair)
 
 
     def spread(value):
         zero = jnp.zeros((width, value.shape[1]), F32)
         return lax.dynamic_update_slice_in_dim(zero, value, member * part, axis=0)
 
-    vec_low = jnp.concatenate([cols_one[:2], cols_mix[:6], cols_two[:4]], axis=0)
+    vec_low = jnp.concatenate([cols_mix[:6], cols_two[:4]], axis=0)
     vec_head = jnp.concatenate(
         [jnp.sum(extra[:, :2], axis=0), jnp.sum(ends[:, SPAN : SPAN + 2], axis=0)], axis=0
     )
     by_feature = jnp.concatenate([down_grad, up_grad, ddown_grad, vec_low.T], axis=1)
     by_channel = spread(jnp.concatenate([tn(d_decay, dh_all), vec_head.T], axis=1))
-    low, main_got = cube_sum(
+    low = cube_sum(
         jnp.concatenate(
             [to_cube(by_feature), by_channel.reshape(*[2] * len(all_masks), rows, -1)], axis=-1
         ),
         BF16,
-        main_got,
-    )
+    )
+    low_one = cube_sum(to_cube(cols_one[:2].T), F32)
     main_sum = far_add(main_kept, main_got)
 
     holder = lax.div(me * rows, part)
@@ -1393,12 +1392,17 @@
         axis=1,
     ).astype(F32)
 
-    vec_at = decay_up + 12
+    vec_at = decay_up + 10
     lowrank_gradient = jnp.concatenate(
         [low[:, :decay_up], low[:, vec_at : vec_at + DRANK]], axis=1
     )
     vectors_gradient = jnp.concatenate(
-        [low[:, decay_up : decay_up + 8], low[:, vec_at + DRANK :], low[:, decay_up + 8 : vec_at]],
+        [
+            low_one,
+            low[:, decay_up : decay_up + 6],
+            low[:, vec_at + DRANK :],
+            low[:, decay_up + 6 : vec_at],
+        ],
         axis=1,
     )
     return (

time: 939 us -> 937 us (level)
  waiting for transfers between devices: 440 us -> 425 us
  starting transfers between devices: 63.4 us -> 74.5 us
    ppermute x63 -> x68, waiting for transfers between devices: 409 us -> 396 us  [trade(): return lax.ppermute(value, 'seq', [(d, d ^ mask) for d in range(count)])]
    ppermute x63 -> x68, starting transfers between devices: 55.9 us -> 67 us  [trade(): return lax.ppermute(value, 'seq', [(d, d ^ mask) for d in range(count)])]
    unnamed x227 -> x247, local copies, waits for them, and re-layouts: 42.7 us -> 39.1 us
  transfers between devices with their start and end apart: 75 -> 80, of which waited for: 49 -> 46; matrix products, arithmetic and copies ran while one was open for 9% -> 10% of each run, Pallas kernels for 26% -> 26%
where the time goes in v2:
time: 937 us; the launch traced here: 926 us
  waiting for transfers between devices  425 us (45%)
  Pallas kernels  268 us (29%)
  local copies, waits for them, and re-layouts  80.7 us (9%)
  starting transfers between devices  74.5 us (8%)
  other arithmetic  60.6 us (6%)
  between operations  16.5 us (2%)
    ppermute x68, waiting for transfers between devices, trade(): return lax.ppermute(value, 'seq', [(d, d ^ mask) for d in range(count)])  396 us
    pallas_call x12, Pallas kernels, product(): pl.pallas_call(kernel, grid=(outs[0][1] // tile,), in_specs=specs, out_sp...  80 us
    pallas_call x24, Pallas kernels, local(): pl.pallas_call(kernel, in_specs=specs, out_specs=[pl.BlockSpec(memory_spa...  72.9 us
    ppermute x68, starting transfers between devices, trade(): return lax.ppermute(value, 'seq', [(d, d ^ mask) for d in range(count)])  67 us
    pallas_call x4, Pallas kernels, block_call(): pl.pallas_call(kernel, grid=(chunks, width // lane), in_specs=[kinds[kind...  48.1 us
    unnamed x247, local copies, waits for them, and re-layouts  39.1 us
    pallas_call x4, Pallas kernels, weight_grad(): pl.pallas_call(kernel, grid_spec=pltpu.PrefetchScalarGridSpec(num_scalar_...  34.8 us
    all_gather x4, waiting for transfers between devices, gather_square(): lax.all_gather(paired, 'seq', axis=0, tiled=True, axis_index_groups=groups)  24.3 us
  transfers between devices with their start and end apart: 80, of which 46 were waited for; matrix products, arithmetic and copies ran while one was open for 10% of the time, Pallas kernels for 26%

profile of v2, /device:TPU:0, one launch (start us, length us, event | category | flops | bytes accessed | tf_op | source)
XLA Modules:
  0.0 925.6 jit_solution(6258433306796879741)
XLA Ops:
  25.1 13.4 %collective-permute-done.4 = f32[2,64,144]{2,1,0:T(8,128)S(1)} collective-permute-done((f32[2,64,144]{2,1,0:T(8,128)S(1)}, f32[2,64,144]{2,1,0:T(8,128)S(1)}, u32[]{:S(2)}, u32[]{:S(2)}) %collective-permute-start.4) | collective-permute-done | bytes 73760 | tf_op jit(solution)/shard_map/ppermute | solution.py:667
  52.9 9.9 %collective-permute-done.8 = f32[2,2,2,64,144]{4,3,2,1,0:T(8,128)S(1)} collective-permute-done((f32[2,2,2,64,144]{4,3,2,1,0:T(8,128)S(1)}, f32[2,2,2,64,144]{4,3,2,1,0:T(8,128)S(1)}, u32[]{:S(2)}, u32[]{:S(2)}) %collective-permute-start.8) | collective-permute-done | bytes 294944 | tf_op jit(solution)/shard_map/ppermute | solution.py:667
  76.8 24.0 %collective-permute-done.15 = bf16[256,1024]{1,0:T(8,128)(2,1)S(1)} collective-permute-done((bf16[256,1024]{1,0:T(8,128)(2,1)S(1)}, bf16[256,1024]{1,0:T(8,128)(2,1)S(1)}, u32[]{:S(2)}, u32[]{:S(2)}) %collective-permute-start.15) | collective-permute-done | bytes 524320 | tf_op jit(solution)/shard_map/ppermute | solution.py:667
  110.1 16.4 %shard_map.137 = (bf16[512,2048]{1,0:T(8,128)(2,1)}, bf16[512,2048]{1,0:T(8,128)(2,1)}, bf16[512,2048]{1,0:T(8,128)(2,1)}, bf16[512,2048]{1,0:T(8,128)(2,1)}, bf...) custom-call(s32[4]{0:T(128)} %add_convert_fusion.4.open_ref, ...), custom_call_target="tpu_custom_call" | custom-call | tf_op jit(solution)/shard_map/pallas_call | solution.py:386
  126.5 12.2 %collective-permute-done.16 = bf16[256,1536]{1,0:T(8,128)(2,1)} collective-permute-done((bf16[256,1536]{1,0:T(8,128)(2,1)S(1)}, bf16[256,1536]{1,0:T(8,128)(2,1)}, u32[]{:S(2)}, u32[]{:S(2)}) %collective-permute-start.16) | collective-permute-done | bytes 786464 | tf_op jit(solution)/shard_map/ppermute | solution.py:667
  142.5 23.9 %collective-permute-done.17 = bf16[128,4096]{1,0:T(8,128)(2,1)S(1)} collective-permute-done((bf16[128,4096]{1,0:T(8,128)(2,1)S(1)}, bf16[128,4096]{1,0:T(8,128)(2,1)S(1)}, u32[]{:S(2)}, u32[]{:S(2)}) %collective-permute-start.17) | collective-permute-done | bytes 1048608 | tf_op jit(solution)/shard_map/ppermute | solution.py:667
  200.1 8.3 collective-permute-done.19.refs_3_
  211.3 22.2 %collective-permute-done.20 = bf16[256,2304]{1,0:T(8,128)(2,1)} collective-permute-done((bf16[256,2304]{1,0:T(8,128)(2,1)}, bf16[256,2304]{1,0:T(8,128)(2,1)}, u32[]{:S(2)}, u32[]{:S(2)}) %collective-permute-start.20) | collective-permute-done | bytes 1179680 | tf_op jit(solution)/shard_map/ppermute | solution.py:667
  263.7 14.3 %shard_map.146 = (f32[512,512]{1,0:T(8,128)S(1)}, bf16[512,512]{1,0:T(8,128)(2,1)S(1)}) custom-call(f32[512,512]{1,0:T(8,128)S(1)} %copy-done.9, f32[512,512]{1,0:T(8,128)S(1)} %copy-done.7, f32[512,512]{1,0:T(8,128)S(1)} %copy-done.8, f32[512,512]{1,0:T(8,128)} %shard_map.140.w_ref, f32[512,512]{1,0:T(8,128)} %get-tuple-element.174.g_ref, ...), custom_call_target="tpu_custom_call" | custom-call | tf_op jit(solution)/shard_map/pallas_call | solution.py:222
  279.8 16.6 %collective-permute-done.23 = bf16[256,1792]{1,0:T(8,128)(2,1)} collective-permute-done((bf16[256,1792]{1,0:T(8,128)(2,1)S(1)}, bf16[256,1792]{1,0:T(8,128)(2,1)}, u32[]{:S(2)}, u32[]{:S(2)}) %collective-permute-start.23) | collective-permute-done | bytes 917536 | tf_op jit(solution)/shard_map/ppermute | solution.py:667
  311.1 14.2 %collective-permute-done.25.refs_2_ = bf16[128,2048]{1,0:T(8,128)(2,1)S(1)} collective-permute-done((bf16[128,2048]{1,0:T(8,128)(2,1)}, bf16[128,2048]{1,0:T(8,128)(2,1)S(1)}, u32[]{:S(2)}, u32[]{:S(2)}) %collective-permute-start.25) | collective-permute-done | bytes 524320 | tf_op jit(solution)/shard_map/ppermute | solution.py:667
  341.9 12.7 %collective-permute-done.27.refs_1_ = bf16[128,2048]{1,0:T(8,128)(2,1)S(1)} collective-permute-done((bf16[128,2048]{1,0:T(8,128)(2,1)S(1)}, bf16[128,2048]{1,0:T(8,128)(2,1)S(1)}, u32[]{:S(2)}, u32[]{:S(2)}) %collective-permute-start.27) | collective-permute-done | bytes 524320 | tf_op jit(solution)/shard_map/ppermute | solution.py:667
  354.8 10.2 %collective-permute-done.29.refs_1_ = bf16[128,2048]{1,0:T(8,128)(2,1)S(1)} collective-permute-done((bf16[128,2048]{1,0:T(8,128)(2,1)S(1)}, bf16[128,2048]{1,0:T(8,128)(2,1)S(1)}, u32[]{:S(2)}, u32[]{:S(2)}) %collective-permute-start.29) | collective-permute-done | bytes 524320 | tf_op jit(solution)/shard_map/ppermute | solution.py:667
  380.6 9.0 shard_map.152
  389.5 24.3 %all-gather.11.cloned.1.call-done.refs_1_ = bf16[2048,1792]{1,0:T(8,128)(2,1)} async-done(((bf16[512,1792]{1,0:T(8,128)(2,1)}), bf16[2048,1792]{1,0:T(8,128)(2,1)}) %all-gather.11.cloned.1.call-update) | async-done | bytes 7340048 | tf_op jit(solution)/shard_map/all_gather | solution.py:775
  413.8 8.3 shard_map.155
  437.5 12.2 %collective-permute-done.32.more_ref = bf16[128,2048]{1,0:T(8,128)(2,1)S(1)} collective-permute-done((bf16[128,2048]{1,0:T(8,128)(2,1)}, bf16[128,2048]{1,0:T(8,128)(2,1)S(1)}, u32[]{:S(2)}, u32[]{:S(2)}) %collective-permute-start.32) | collective-permute-done | bytes 524320 | tf_op jit(solution)/shard_map/ppermute | solution.py:667
  457.5 12.0 %collective-permute-done.35.refs_1_ = bf16[128,2048]{1,0:T(8,128)(2,1)S(1)} collective-permute-done((bf16[128,2048]{1,0:T(8,128)(2,1)}, bf16[128,2048]{1,0:T(8,128)(2,1)S(1)}, u32[]{:S(2)}, u32[]{:S(2)}) %collective-permute-start.35) | collective-permute-done | bytes 524320 | tf_op jit(solution)/shard_map/ppermute | solution.py:667
  490.1 9.0 shard_map.160.refs_1_.refs_0_
  508.6 8.3 shard_map.162
  532.9 8.8 collective-permute-done.40.refs_1_
  541.7 10.9 %collective-permute-done.42.refs_3_ = bf16[128,2048]{1,0:T(8,128)(2,1)S(1)} collective-permute-done((bf16[128,2048]{1,0:T(8,128)(2,1)}, bf16[128,2048]{1,0:T(8,128)(2,1)S(1)}, u32[]{:S(2)}, u32[]{:S(2)}) %collective-permute-start.42) | collective-permute-done | bytes 524320 | tf_op jit(solution)/shard_map/ppermute | solution.py:667
  569.1 11.3 %collective-permute-done.44.refs_1_ = bf16[128,2048]{1,0:T(8,128)(2,1)S(1)} collective-permute-done((bf16[128,2048]{1,0:T(8,128)(2,1)}, bf16[128,2048]{1,0:T(8,128)(2,1)S(1)}, u32[]{:S(2)}, u32[]{:S(2)}) %collective-permute-start.44) | collective-permute-done | bytes 524320 | tf_op jit(solution)/shard_map/ppermute | solution.py:667
  597.8 12.2 %shard_map.170 = (bf16[512,512]{1,0:T(8,128)(2,1)S(1)}, f32[512,512]{1,0:T(8,128)S(1)}, f32[4,72,512]{2,1,0:T(8,128)S(1)}) custom-call(f32[512,512]{1,0:T(8,128)S(1)} %copy-done.15, f32[512,512]{1,0:T(8,128)S(1)} %copy-done.16, f32[512,512]{1,0:T(8,128)S(1)} %copy-done.29, f32[512,512]{1,0:T(8,128)} %get-tuple-element.165.r_ref, ...), custom_call_target="tpu_custom_call" | custom-call | tf_op jit(solution)/shard_map/pallas_call | solution.py:222
  642.0 9.4 %shard_map.175 = bf16[8,256,1536]{2,1,0:T(8,128)(2,1)} custom-call(s32[8]{0:T(128)S(1)} %iota.14._, bf16[512,2048]{1,0:T(8,128)(2,1)S(1)} %copy-done.4, bf16[512,512]{1,0:T(8,128)(2,1)S(1)} %copy-done.27, bf16[512,2048]{1,0:T(8,128)(2,1)S(1)} %copy-done.2, bf16[512,512]{1,0:T(8,128)(2,1)S(1)} %copy-done.14, ...), custom_call_target="tpu_custom_call" | custom-call | tf_op jit(solution)/shard_map/pallas_call | solution.py:248
  661.6 14.8 %shard_map.176 = (bf16[512,512]{1,0:T(8,128)(2,1)S(1)}, bf16[512,512]{1,0:T(8,128)(2,1)S(1)}, bf16[512,512]{1,0:T(8,128)(2,1)S(1)}, bf16[512,512]{1,0:T(8,128)(2,1)S(1)}, f32[4,8,512]{2,1,0:T(8,128)S(1)}) custom-call(f32[512,512]{1,0:T(8,128)S(1)} %copy-done.10, f32[512,512]{1,0:T(8,128)S(1)} %copy-done.7, f32[512,512]{1,0:T(8,128)} %get-tuple-element.172.v_ref, ...), custom_call_target="tpu_custom_call" | custom-call | tf_op jit(solution)/shard_map/pallas_call | solution.py:222
  686.6 9.4 %shard_map.178 = bf16[8,256,1536]{2,1,0:T(8,128)(2,1)} custom-call(s32[8]{0:T(128)S(1)} %iota.15._, bf16[512,2048]{1,0:T(8,128)(2,1)S(1)} %copy-done.11, bf16[512,512]{1,0:T(8,128)(2,1)S(1)} %get-tuple-element.250.refs_0_.refs_1_, bf16[512,2048]{1,0:T(8,128)(2,1)S(1)} %copy-done.12, bf16[512,512]{1,0:T(8,128)(2,1)S(1)} %get-tuple-element.251.refs_2_.refs_3_, ...), custom_call_target="tpu_custom_call" | custom-call | tf_op jit(solution)/shard_map/pallas_call | solution.py:248
  696.1 11.1 %shard_map.177 = (f32[1024,2048]{1,0:T(8,128)}, bf16[1024,2048]{1,0:T(8,128)(2,1)}) custom-call(bf16[512,512]{1,0:T(8,128)(2,1)} %copy-done.20, bf16[2048,1024]{1,0:T(8,128)(2,1)} %all-gather.7.cloned.1.call-done.refs_1_.refs_3_, bf16[512,512]{1,0:T(8,128)(2,1)} %copy-done.21, bf16[2048,1024]{1,0:T(8,128)(2,1)} %all-gather.7.cloned.1.call-done.refs_1_.refs_3_, ...), custom_call_target="tpu_custom_call" | custom-call | tf_op jit(solution)/shard_map/pallas_call | solution.py:428
  723.0 11.4 %collective-permute-done.54 = bf16[128,3584]{1,0:T(8,128)(2,1)S(1)} collective-permute-done((bf16[128,3584]{1,0:T(8,128)(2,1)S(1)}, bf16[128,3584]{1,0:T(8,128)(2,1)S(1)}, u32[]{:S(2)}, u32[]{:S(2)}) %collective-permute-start.54) | collective-permute-done | bytes 917536 | tf_op jit(solution)/shard_map/ppermute | solution.py:667
  750.6 56.7 %collective-permute-done.55.got_ref = bf16[512,2048]{1,0:T(8,128)(2,1)} collective-permute-done((bf16[512,2048]{1,0:T(8,128)(2,1)}, bf16[512,2048]{1,0:T(8,128)(2,1)}, u32[]{:S(2)}, u32[]{:S(2)}) %collective-permute-start.55) | collective-permute-done | bytes 2097184 | tf_op jit(solution)/shard_map/ppermute | solution.py:667
  807.3 11.7 %shard_map.182 = (f32[128,2048]{1,0:T(8,128)}, f32[128,2048]{1,0:T(8,128)}, f32[8,2048]{1,0:T(8,128)}, f32[8,2048]{1,0:T(8,128)}, f32[2048,160]{1,0:T(8,128)}, /*index=5*/f32[2048,160]{1,0:T(8,128)}, f32[2048,64]{1,0:T(8,128)}) custom-call(f32[512,2048]{1,0:T(8,128)} %get-tuple-element.261.kept_ref, bf16[512,2048]{1,0:T(8,128)(2,1)} %collective-permute-done.55.got_ref, ...), custom_call_target="tpu_custom_call" | custom-call | tf_op jit(solution)/shard_map/pallas_call | solution.py:597
  835.0 23.4 %collective-permute-done.57 = bf16[256,1536]{1,0:T(8,128)(2,1)} collective-permute-done((bf16[256,1536]{1,0:T(8,128)(2,1)}, bf16[256,1536]{1,0:T(8,128)(2,1)}, u32[]{:S(2)}, u32[]{:S(2)}) %collective-permute-start.57) | collective-permute-done | bytes 786464 | tf_op jit(solution)/shard_map/ppermute | solution.py:667
  (603 shorter events, 436.8 us)
Async XLA Ops:
  7.2 164.4 %all-gather.7.cloned.1.call-start = ((), (), s32[]{:S(2)}) async-start(), calls=%async_computation.5 | async-start | bytes 5242880 | tf_op jit(solution)/shard_map/all_gather | solution.py:775
  18.7 44.4 %collective-permute-start.13 = (bf16[144,2048]{1,0:T(8,128)(2,1)S(1)}, bf16[144,2048]{1,0:T(8,128)(2,1)S(1)}, u32[]{:S(2)}, u32[]{:S(2)}) collective-permute-start(bf16[144,2048]{1,0:T(8,128)(2,1)S(1)} %shard_map.135.refs_0_), channel_id=1, source_target_pairs={{0,8},{1,9},{2,10},{3,11},{4,12},{5,13},{6,14},{7,15},{8,0},{9,1},... | collective-permute-start | bytes 1769480 | tf_op jit(solution)/shard_map/ppermute | solution.py:667
  24.7 15.9 %collective-permute-start.2 = (bf16[2,64,384]{2,1,0:T(8,128)(2,1)S(1)}, bf16[2,64,384]{2,1,0:T(8,128)(2,1)S(1)}, u32[]{:S(2)}, u32[]{:S(2)}) collective-permute-start(bf16[2,64,384]{2,1,0:T(8,128)(2,1)S(1)} %pad_maximum_fusion.35), channel_id=1, source_target_pairs={{0,8},{1,9},{2,10},{3,11},{4,12},{5,13},{6,14},{7,15},{8,0},{9,1},... | collective-permute-start | bytes 294920 | tf_op jit(solution)/shard_map/ppermute | solution.py:667
  40.9 22.8 %collective-permute-start.5 = (bf16[128,2560]{1,0:T(8,128)(2,1)S(1)}, bf16[128,2560]{1,0:T(8,128)(2,1)S(1)}, u32[]{:S(2)}, u32[]{:S(2)}) collective-permute-start(bf16[128,2560]{1,0:T(8,128)(2,1)S(1)} %pad_maximum_fusion.20), channel_id=1, source_target_pairs={{0,8},{1,9},{2,10},{3,11},{4,12},{5,13},{6,14},{7,15},{8,0},{9,1},... | collective-permute-start | bytes 1966088 | tf_op jit(solution)/shard_map/ppermute | solution.py:667
  51.3 17.5 %collective-permute-start.11 = (bf16[2,2,2,64,384]{4,3,2,1,0:T(8,128)(2,1)S(1)}, bf16[2,2,2,64,384]{4,3,2,1,0:T(8,128)(2,1)S(1)}, u32[]{:S(2)}, u32[]{:S(2)}) collective-permute-start(bf16[2,2,2,64,384]{4,3,2,1,0:T(8,128)(2,1)S(1)} %pad_maximum_fusion.27), channel_id=1, source_target_pairs={{0,2},{1,3},{2,0},{3,1},{4,6},{5,7},{6,4},{7,5},{8,10},{9,11},{10,... | collective-permute-start | bytes 1179656 | tf_op jit(solution)/shard_map/ppermute | solution.py:667
  74.6 26.2 %collective-permute-start.15 = (bf16[256,1024]{1,0:T(8,128)(2,1)S(1)}, bf16[256,1024]{1,0:T(8,128)(2,1)S(1)}, u32[]{:S(2)}, u32[]{:S(2)}) collective-permute-start(bf16[256,1024]{1,0:T(8,128)(2,1)S(1)} %slice.303), channel_id=1, source_target_pairs={{0,16},{1,17},{2,18},{3,19},{4,20},{5,21},{6,22},{7,23},{8,24},{9,... | collective-permute-start | bytes 1572872 | tf_op jit(solution)/shard_map/ppermute | solution.py:667
  102.0 154.0 %all-gather.5.cloned.1.call-start = ((), (), s32[]{:S(2)}) async-start(), calls=%async_computation.4 | async-start | bytes 7864320 | tf_op jit(solution)/shard_map/all_gather | solution.py:775
  102.0 36.7 %collective-permute-start.16 = (bf16[256,1536]{1,0:T(8,128)(2,1)S(1)}, bf16[256,1536]{1,0:T(8,128)(2,1)}, u32[]{:S(2)}, u32[]{:S(2)}) collective-permute-start(bf16[256,1536]{1,0:T(8,128)(2,1)S(1)} %slice.304), channel_id=1, source_target_pairs={{0,16},{1,17},{2,18},{3,19},{4,20},{5,21},{6,22},{7,23},{8,24},{9,... | collective-permute-start | bytes 2359304 | tf_op jit(solution)/shard_map/ppermute | solution.py:667
  141.2 232.0 %all-gather.9.cloned.1.call-start = ((), (), s32[]{:S(2)}) async-start(), calls=%async_computation.6 | async-start | bytes 11796480 | tf_op jit(solution)/shard_map/all_gather | solution.py:775
  142.4 24.0 %collective-permute-start.17 = (bf16[128,4096]{1,0:T(8,128)(2,1)S(1)}, bf16[128,4096]{1,0:T(8,128)(2,1)S(1)}, u32[]{:S(2)}, u32[]{:S(2)}) collective-permute-start(bf16[128,4096]{1,0:T(8,128)(2,1)S(1)} %maximum_maximum_fusion), channel_id=1, source_target_pairs={{0,8},{1,9},{2,10},{3,11},{4,12},{5,13},{6,14},{7,15},{8,0},{9,1},... | collective-permute-start | bytes 3145736 | tf_op jit(solution)/shard_map/ppermute | solution.py:667
  179.3 54.2 %collective-permute-start.20 = (bf16[256,2304]{1,0:T(8,128)(2,1)}, bf16[256,2304]{1,0:T(8,128)(2,1)}, u32[]{:S(2)}, u32[]{:S(2)}) collective-permute-start(bf16[256,2304]{1,0:T(8,128)(2,1)} %slice.312), channel_id=1, source_target_pairs={{0,16},{1,17},{2,18},{3,19},{4,20},{5,21},{6,22},{7,23},{8,24},{9,... | collective-permute-start | bytes 3538952 | tf_op jit(solution)/shard_map/ppermute | solution.py:667
  236.6 177.2 %all-gather.11.cloned.1.call-start = ((), (), s32[]{:S(2)}) async-start(), calls=%async_computation.7 | async-start | bytes 9175040 | tf_op jit(solution)/shard_map/all_gather | solution.py:775
  255.4 41.0 %collective-permute-start.23 = (bf16[256,1792]{1,0:T(8,128)(2,1)S(1)}, bf16[256,1792]{1,0:T(8,128)(2,1)}, u32[]{:S(2)}, u32[]{:S(2)}) collective-permute-start(bf16[256,1792]{1,0:T(8,128)(2,1)S(1)} %slice.314), channel_id=1, source_target_pairs={{0,16},{1,17},{2,18},{3,19},{4,20},{5,21},{6,22},{7,23},{8,24},{9,... | collective-permute-start | bytes 2752520 | tf_op jit(solution)/shard_map/ppermute | solution.py:667
  299.1 284.6 %reduce-scatter.5.cloned.1.call-start = ((), (), s32[]{:S(2)}) async-start(), calls=%async_computation.8 | async-start | bytes 9175040 | tf_op jit(solution)/shard_map/reduce_scatter | solution.py:785
  336.3 18.3 %collective-permute-start.27 = (bf16[128,2048]{1,0:T(8,128)(2,1)S(1)}, bf16[128,2048]{1,0:T(8,128)(2,1)S(1)}, u32[]{:S(2)}, u32[]{:S(2)}) collective-permute-start(bf16[128,2048]{1,0:T(8,128)(2,1)S(1)} %get-tuple-element.389.refs_0_), channel_id=1, source_target_pairs={{0,8},{1,9},{2,10},{3,11},{4,12},{5,13},{6,14},{7,15},{8,0},{9,1},... | collective-permute-start | bytes 1572872 | tf_op jit(solution)/shard_map/ppermute | solution.py:667
  341.9 23.1 %collective-permute-start.29 = (bf16[128,2048]{1,0:T(8,128)(2,1)S(1)}, bf16[128,2048]{1,0:T(8,128)(2,1)S(1)}, u32[]{:S(2)}, u32[]{:S(2)}) collective-permute-start(bf16[128,2048]{1,0:T(8,128)(2,1)S(1)} %get-tuple-element.388.refs_0_), channel_id=1, source_target_pairs={{0,8},{1,9},{2,10},{3,11},{4,12},{5,13},{6,14},{7,15},{8,0},{9,1},... | collective-permute-start | bytes 1572872 | tf_op jit(solution)/shard_map/ppermute | solution.py:667
  456.9 16.9 %collective-permute-start.37 = (bf16[256,512]{1,0:T(8,128)(2,1)S(1)}, bf16[256,512]{1,0:T(8,128)(2,1)S(1)}, u32[]{:S(2)}, u32[]{:S(2)}) collective-permute-start(bf16[256,512]{1,0:T(8,128)(2,1)S(1)} %concatenate.199), channel_id=1, source_target_pairs={{0,8},{1,9},{2,10},{3,11},{4,12},{5,13},{6,14},{7,15},{8,0},{9,1},... | collective-permute-start | bytes 786440 | tf_op jit(solution)/shard_map/ppermute | solution.py:667
  490.0 166.8 %reduce-scatter.7.cloned.1.call-start = ((), (), s32[]{:S(2)}) async-start(), calls=%async_computation.9 | async-start | bytes 9175040 | tf_op jit(solution)/shard_map/reduce_scatter | solution.py:785
  508.6 239.0 %reduce-scatter.9.cloned.1.call-start = ((), (), s32[]{:S(2)}) async-start(), calls=%async_computation.10 | async-start | bytes 7864320 | tf_op jit(solution)/shard_map/reduce_scatter | solution.py:785
  532.5 20.1 %collective-permute-start.42 = (bf16[128,2048]{1,0:T(8,128)(2,1)}, bf16[128,2048]{1,0:T(8,128)(2,1)S(1)}, u32[]{:S(2)}, u32[]{:S(2)}) collective-permute-start(bf16[128,2048]{1,0:T(8,128)(2,1)} %get-tuple-element.222), channel_id=1, source_target_pairs={{0,8},{1,9},{2,10},{3,11},{4,12},{5,13},{6,14},{7,15},{8,0},{9,1},... | collective-permute-start | bytes 1572872 | tf_op jit(solution)/shard_map/ppermute | solution.py:667
  585.9 43.5 %collective-permute-start.47 = (bf16[256,1792]{1,0:T(8,128)(2,1)}, bf16[256,1792]{1,0:T(8,128)(2,1)}, u32[]{:S(2)}, u32[]{:S(2)}) collective-permute-start(bf16[256,1792]{1,0:T(8,128)(2,1)} %constant_dynamic-slice_fusion.13), channel_id=1, source_target_pairs={{0,16},{1,17},{2,18},{3,19},{4,20},{5,21},{6,22},{7,23},{8,24},{9,... | collective-permute-start | bytes 2752520 | tf_op jit(solution)/shard_map/ppermute | solution.py:667
  654.1 164.9 %reduce-scatter.11.cloned.1.call-start = ((), (), s32[]{:S(2)}) async-start(), calls=%async_computation.11 | async-start | bytes 7864320 | tf_op jit(solution)/shard_map/reduce_scatter | solution.py:785
  658.9 48.2 %collective-permute-start.52 = (bf16[256,1792]{1,0:T(8,128)(2,1)}, bf16[256,1792]{1,0:T(8,128)(2,1)}, u32[]{:S(2)}, u32[]{:S(2)}) collective-permute-start(bf16[256,1792]{1,0:T(8,128)(2,1)} %constant_dynamic-slice_fusion.12), channel_id=1, source_target_pairs={{0,16},{1,17},{2,18},{3,19},{4,20},{5,21},{6,22},{7,23},{8,24},{9,... | collective-permute-start | bytes 2752520 | tf_op jit(solution)/shard_map/ppermute | solution.py:667
  683.3 23.9 %collective-permute-start.51 = (bf16[128,64]{1,0:T(8,128)(2,1)}, bf16[128,64]{1,0:T(8,128)(2,1)S(1)}, u32[]{:S(2)}, u32[]{:S(2)}) collective-permute-start(bf16[128,64]{1,0:T(8,128)(2,1)} %get-tuple-element.258), channel_id=1, source_target_pairs={{0,8},{1,9},{2,10},{3,11},{4,12},{5,13},{6,14},{7,15},{8,0},{9,1},... | collective-permute-start | bytes 49160 | tf_op jit(solution)/shard_map/ppermute | solution.py:667
  711.5 23.0 %collective-permute-start.54 = (bf16[128,3584]{1,0:T(8,128)(2,1)S(1)}, bf16[128,3584]{1,0:T(8,128)(2,1)S(1)}, u32[]{:S(2)}, u32[]{:S(2)}) collective-permute-start(bf16[128,3584]{1,0:T(8,128)(2,1)S(1)} %pad_maximum_fusion.15), channel_id=1, source_target_pairs={{0,8},{1,9},{2,10},{3,11},{4,12},{5,13},{6,14},{7,15},{8,0},{9,1},... | collective-permute-start | bytes 2752520 | tf_op jit(solution)/shard_map/ppermute | solution.py:667
  742.0 65.2 %collective-permute-start.55 = (bf16[512,2048]{1,0:T(8,128)(2,1)}, bf16[512,2048]{1,0:T(8,128)(2,1)}, u32[]{:S(2)}, u32[]{:S(2)}) collective-permute-start(bf16[512,2048]{1,0:T(8,128)(2,1)} %get-tuple-element.265), channel_id=1, source_target_pairs={{0,8},{1,9},{2,10},{3,11},{4,12},{5,13},{6,14},{7,15},{8,0},{9,1},... | collective-permute-start | bytes 6291464 | tf_op jit(solution)/shard_map/ppermute | solution.py:667
  748.9 58.4 %collective-permute-start.56 = (bf16[256,1536]{1,0:T(8,128)(2,1)S(1)}, bf16[256,1536]{1,0:T(8,128)(2,1)}, u32[]{:S(2)}, u32[]{:S(2)}) collective-permute-start(bf16[256,1536]{1,0:T(8,128)(2,1)S(1)} %constant_dynamic-slice_fusion.11), channel_id=1, source_target_pairs={{0,16},{1,17},{2,18},{3,19},{4,20},{5,21},{6,22},{7,23},{8,24},{9,... | collective-permute-start | bytes 2359304 | tf_op jit(solution)/shard_map/ppermute | solution.py:667
  821.2 37.2 %collective-permute-start.57 = (bf16[256,1536]{1,0:T(8,128)(2,1)}, bf16[256,1536]{1,0:T(8,128)(2,1)}, u32[]{:S(2)}, u32[]{:S(2)}) collective-permute-start(bf16[256,1536]{1,0:T(8,128)(2,1)} %constant_dynamic-slice_fusion.10), channel_id=1, source_target_pairs={{0,16},{1,17},{2,18},{3,19},{4,20},{5,21},{6,22},{7,23},{8,24},{9,... | collective-permute-start | bytes 2359304 | tf_op jit(solution)/shard_map/ppermute | solution.py:667
  822.4 36.0 %collective-permute-start.58 = (f32[8,2048]{1,0:T(8,128)}, f32[8,2048]{1,0:T(8,128)S(1)}, u32[]{:S(2)}, u32[]{:S(2)}) collective-permute-start(f32[8,2048]{1,0:T(8,128)} %get-tuple-element.281), channel_id=1, source_target_pairs={{1,0},{2,1},{3,2},{4,3},{5,4},{6,5},{7,6},{8,7},{9,8},{10,9},{11,1... | collective-permute-start | bytes 196616 | tf_op jit(solution)/shard_map/ppermute | solution.py:738
  832.5 39.1 %collective-permute-start.61 = (bf16[2,2,2,2,64,462]{5,4,3,2,1,0:T(8,128)(2,1)}, bf16[2,2,2,2,64,462]{5,4,3,2,1,0:T(8,128)(2,1)}, u32[]{:S(2)}, u32[]{:S(2)}) collective-permute-start(bf16[2,2,2,2,64,462]{5,4,3,2,1,0:T(8,128)(2,1)} %fusion.5), channel_id=1, source_target_pairs={{0,1},{1,0},{2,3},{3,2},{4,5},{5,4},{6,7},{7,6},{8,9},{9,8},{10,11... | collective-permute-start | bytes 2838536 | tf_op jit(solution)/shard_map/ppermute | solution.py:667
  876.4 21.2 %collective-permute-start.59 = (bf16[128,3200]{1,0:T(8,128)(2,1)}, bf16[128,3200]{1,0:T(8,128)(2,1)}, u32[]{:S(2)}, u32[]{:S(2)}) collective-permute-start(bf16[128,3200]{1,0:T(8,128)(2,1)} %pad_maximum_fusion.17), channel_id=1, source_target_pairs={{0,8},{1,9},{2,10},{3,11},{4,12},{5,13},{6,14},{7,15},{8,0},{9,1},... | collective-permute-start | bytes 2457608 | tf_op jit(solution)/shard_map/ppermute | solution.py:667
  880.6 15.9 %collective-permute-start.69 = (f32[2,64,2]{1,2,0:T(2,128)S(1)}, f32[2,64,2]{1,2,0:T(2,128)S(1)}, u32[]{:S(2)}, u32[]{:S(2)}) collective-permute-start(f32[2,64,2]{1,2,0:T(2,128)S(1)} %fusion.30), channel_id=1, source_target_pairs={{0,8},{1,9},{2,10},{3,11},{4,12},{5,13},{6,14},{7,15},{8,0},{9,1},... | collective-permute-start | bytes 3080 | tf_op jit(solution)/shard_map/ppermute | solution.py:667
  (155 other events, 1366.8 us)
Sparse Core Ops, SparseCore 0:
  102.1 52.3 all-gather.6
  156.4 73.7 all-gather.4
  236.7 96.4 all-gather.8
  334.9 78.8 all-gather.10
  490.1 79.4 reduce-scatter.4
  572.5 84.2 reduce-scatter.6
  659.7 70.2 reduce-scatter.8
  733.0 70.2 reduce-scatter.10
